TPU v7x, 128 devices: a whole 4x4x4 slice. The times are simulated.
128 devices in a mesh: replica: 8 (over z_lo, x), mp: 16 (over z_hi, y, core).
Axes of the slice: x: 4, y: 4, z: 4 (z_hi: 2, z_lo: 2; z = z_hi * 2 + z_lo), core: 2. Of those that a mesh axis runs over, the one named last changes fastest.
Arguments:
- indices: int32 [256, 8, 16384], P('mp', None, 'replica'), may hold values from 0 to 511
- lengths: int32 [256, 16384], P('mp', 'replica'), may hold values from 1 to 8
- tables: bfloat16 [256, 512, 256], P('mp'), may hold values from -0.59765625 to 0.59765625
- proj: bfloat16 [256, 16], replicated, may hold values from -0.375 to 0.375
- w_hidden: bfloat16 [4096, 64], replicated, may hold values from -0.75 to 0.75
- w_out: bfloat16 [4096], replicated, may hold values from -0.09375 to 0.09375
- d_logit: float32 [16384], P(('replica', 'mp')), may hold values from -0.375 to 0.375
Outputs:
- logits: float32 [16384], P(('replica', 'mp'))
- table_grad: float32 [256, 512, 256], P('mp')
- hidden_grad: float32 [4096, 64], P(('replica', 'mp'))
- out_grad: float32 [4096], P(('replica', 'mp'))
- proj_grad: float32 [256, 16], P(('replica', 'mp'))
All inputs are finite; a program needn't handle non-finite values.
Results may differ from a plain program's by a relative error of at most 0.035.
Values may be sent and summed in bfloat16 or wider, within the bound.
A program may use at most 192 MiB of HBM per device.

v0:
```python
import jax
import jax.numpy as jnp
from jax import lax
from jax.sharding import PartitionSpec as P

K1 = 8
K2 = 8


def local(indices, lengths, tables, proj, w_hidden, w_out, d_logit):
    highest = lax.Precision.HIGHEST
    fields_here = indices.shape[0]
    bag_slots = indices.shape[1]
    group_rows = indices.shape[2]
    table_rows = tables.shape[1]
    emb_width = tables.shape[2]
    model_size = lax.axis_size("mp")
    local_rows = group_rows // model_size
    row_ids = lax.broadcasted_iota(jnp.int32, (1, table_rows, 1), 1)
    counts = jnp.zeros((fields_here, table_rows, group_rows), jnp.bfloat16)
    for slot_id in range(bag_slots):
        matches = (indices[:, slot_id, None, :] == row_ids) & (lengths[:, None, :] > slot_id)
        counts = counts + matches.astype(jnp.bfloat16)
    pooled = jnp.einsum("frb,fre->fbe", counts, tables, preferred_element_type=jnp.float32).astype(
        jnp.bfloat16
    )
    outgoing = pooled.reshape(fields_here, model_size, local_rows, emb_width)
    fields_all = lax.all_to_all(outgoing, "mp", split_axis=1, concat_axis=0, tiled=True)[:, 0]
    factor_rows = jnp.einsum("fk,fne->kne", proj, fields_all, preferred_element_type=jnp.float32)
    inter = jnp.einsum("ine,jne->ijn", factor_rows[:K1], factor_rows[K1:], precision=highest)
    interaction = inter.reshape(K1 * K2, inter.shape[2])
    features = interaction.astype(jnp.bfloat16)
    pre_act = jnp.dot(w_hidden, features, preferred_element_type=jnp.float32)
    hidden = jax.nn.silu(pre_act).astype(jnp.bfloat16)
    logits = jnp.dot(w_out, hidden, preferred_element_type=jnp.float32)
    out_part = jnp.dot(hidden.astype(jnp.float32), d_logit, precision=highest)
    sigmoid_v = jax.nn.sigmoid(pre_act)
    d_hidden = (
        w_out.astype(jnp.float32)[:, None]
        * d_logit[None, :]
        * sigmoid_v
        * (1.0 + pre_act * (1.0 - sigmoid_v))
    ).astype(jnp.bfloat16)
    hidden_part = lax.dot_general(
        d_hidden, features, (((1,), (1,)), ((), ())), preferred_element_type=jnp.float32
    )
    d_inter = lax.dot_general(
        w_hidden, d_hidden, (((0,), (0,)), ((), ())), preferred_element_type=jnp.float32
    ).reshape(K1, K2, local_rows)
    d_left = jnp.einsum("ijn,jne->ine", d_inter, factor_rows[K1:], precision=highest)
    d_right = jnp.einsum("ijn,ine->jne", d_inter, factor_rows[:K1], precision=highest)
    d_factors = jnp.concatenate([d_left, d_right], axis=0).astype(jnp.bfloat16)
    proj_part = jnp.einsum("fne,kne->fk", fields_all, d_factors, preferred_element_type=jnp.float32)
    d_pooled = jnp.einsum(
        "fk,kne->fne", proj, d_factors, preferred_element_type=jnp.float32
    ).astype(jnp.bfloat16)
    returned = lax.all_to_all(
        d_pooled.reshape(model_size, fields_here, local_rows, emb_width),
        "mp",
        split_axis=0,
        concat_axis=2,
        tiled=True,
    )
    d_rows = returned.reshape(fields_here, group_rows, emb_width)
    table_part = jnp.einsum("frb,fbe->fre", counts, d_rows, preferred_element_type=jnp.float32)
    table_grad = lax.psum(table_part.astype(jnp.bfloat16), "replica").astype(jnp.float32)
    hidden_share, out_share, proj_share = (
        lax.psum_scatter(hidden_part, ("replica", "mp"), scatter_dimension=0, tiled=True),
        lax.psum_scatter(out_part, ("replica", "mp"), scatter_dimension=0, tiled=True),
        lax.psum_scatter(proj_part, ("replica", "mp"), scatter_dimension=0, tiled=True),
    )
    return (logits, table_grad, hidden_share, out_share, proj_share)


def solution(mesh):
    in_specs = (
        P("mp", None, "replica"),
        P("mp", "replica"),
        P("mp", None, None),
        P(),
        P(),
        P(),
        P(("replica", "mp")),
    )
    out_specs = (
        P(("replica", "mp")),
        P("mp", None, None),
        P(("replica", "mp"), None),
        P(("replica", "mp")),
        P(("replica", "mp"), None),
    )
    return jax.shard_map(local, mesh=mesh, in_specs=in_specs, out_specs=out_specs, check_vma=False)
```

profile of v0, /device:TPU:0, one launch (start us, length us, event | category | flops | bytes accessed | tf_op | source)
XLA Modules:
  0.0 1398.6 jit_solution(14172258691490630520)
XLA Ops:
  8.0 1.1 broadcast_compare_fusion.7
  9.2 5.6 fusion.41
  15.3 112.8 %convolution_convert_fusion = bf16[16,2048,256]{2,1,0:T(8,128)(2,1)S(1)} fusion(bf16[16,512,256]{2,1,0:T(8,128)(2,1)} %param.9, s32[16,2048]{1,0:T(8,128)S(1)} %get-tuple-element.25, s32[16,2048]{1,0:T(8,128)S(1)} %get-tuple-element.26, s32[16,2048]{1,0:T(8,128)S(1)} %get-tuple-element.27, s32[16,2048]{1,0:T(8,128)S(1)} %get-tuple-element.28, ...), kind=kOutput, calls=%fused_computation.31 | convolution fusion | flops 9269411840 | bytes 22282240 | tf_op jit(solution)/shard_map/frb,fre->fbe/dot_general | solution.py:24
  128.2 6.6 copy.44
  134.9 8.2 all-to-all-start
  143.0 0.2 all-reduce.5.cloned.1.call-start
  143.3 224.7 %all-to-all-done = bf16[16,16,128,256]{3,2,0,1:T(8,128)(2,1)} async-done(((bf16[16,16,128,256]{3,2,0,1:T(8,128)(2,1)}), bf16[16,16,128,256]{3,2,0,1:T(8,128)(2,1)}, u32[]{:S(2)}, u32[]{:S(2)}) %all-to-all-start) | async-done | bytes 16777248 | tf_op jit(solution)/shard_map/all_to_all | solution.py:28
  368.0 11.7 copy.45
  379.6 5.7 copy-done.2
  385.4 2.3 convolution_bitcast_fusion.1
  387.7 1.1 fusion.25
  389.0 2.2 multiply_convert_fusion
  391.1 1.0 copy-done.3
  392.1 0.5 convolution_bitcast_fusion.3
  392.6 0.2 copy.48
  392.9 1.2 fusion.23
  394.1 1.8 fusion.24
  395.9 9.2 convolution_convert_fusion.1
  405.1 8.2 copy.49
  413.3 192.6 %all_to_all.30 = bf16[16,16,128,256]{3,1,2,0:T(8,128)(2,1)S(1)} all-to-all(bf16[16,16,128,256]{3,1,2,0:T(8,128)(2,1)S(1)} %copy.49), channel_id=1, replica_groups=mesh['replica'=8,'mp'=16] {'mp'}, dimensions={0} | all-to-all | bytes 33554432 | tf_op jit(solution)/shard_map/all_to_all | solution.py:57
  605.9 12.1 copy.50
  618.2 107.8 %convolution_convert_fusion.2 = bf16[16,512,256]{2,1,0:T(8,128)(2,1)} fusion(bf16[16,2048,256]{2,1,0:T(8,128)(2,1)S(1)} %bitcast.81, s32[16,2048]{1,0:T(8,128)S(1)} %get-tuple-element.25, s32[16,2048]{1,0:T(8,128)S(1)} %copy-done.7, s32[16,2048]{1,0:T(8,128)S(1)} %copy-done.9, s32[16,2048]{1,0:T(8,128)S(1)} %copy-done.11, s32[16,2048]{1,0:T(8,128)S(1)} %copy-done.13, ...), kind=kOutput, calls=%fused_computation.34 | convolution fusion | flops 9263120384 | bytes 22282240 | tf_op jit(solution)/shard_map/frb,fbe->fre/dot_general | solution.py:65
  726.1 1.9 fusion.30
  728.0 0.7 reshape.49
  728.7 1.2 fusion.35
  729.9 8.7 convolution_bitcast_fusion.2
  738.6 121.0 %all-reduce.2 = (f32[4096]{0:T(1024)S(1)}, f32[256,16]{1,0:T(8,128)S(1)}) all-reduce(f32[4096]{0:T(1024)S(1)} %bitcast.83, f32[256,16]{1,0:T(8,128)S(1)} %convolution_bitcast_fusion.2), channel_id=3, replica_groups=mesh['replica'=8,'mp'=16] {'replica','mp'}, use_global_device_ids=true, to_apply=%region_2.3.clone | all-reduce | flops 8192 | bytes 65536
  859.7 0.6 dynamic-slice
  860.3 0.6 constant_dynamic-slice_fusion
  860.8 0.9 convolution_bitcast_fusion.4
  861.7 6.5 convert_element_type.77
  868.2 523.0 %reduce-scatter.2.cloned.1.call-done = f32[32,64]{1,0:T(8,128)} async-done(((f32[4096,64]{1,0:T(8,128)}), f32[32,64]{1,0:T(8,128)}) %reduce-scatter.2.cloned.1.call-update) | async-done | bytes 8208 | tf_op jit(solution)/shard_map/reduce_scatter | solution.py:68
  (82 shorter events, 0.8 us)
Async XLA Ops:
  8.0 380.9 %copy-start = (bf16[4096,64]{0,1:T(8,128)(2,1)S(1)}, bf16[4096,64]{0,1:T(8,128)(2,1)}, u32[]{:S(2)}) copy-start(bf16[4096,64]{0,1:T(8,128)(2,1)} %param.11) | copy-start | bytes 1572868
  9.2 119.0 %copy-start.19 = (pred[16,2048]{1,0:T(8,128)(4,1)}, pred[16,2048]{1,0:T(8,128)(4,1)S(1)}, u32[]{:S(2)}) copy-start(pred[16,2048]{1,0:T(8,128)(4,1)S(1)} %get-tuple-element.17) | copy-start | bytes 98308
  9.2 119.0 %copy-start.21 = (pred[16,2048]{1,0:T(8,128)(4,1)}, pred[16,2048]{1,0:T(8,128)(4,1)S(1)}, u32[]{:S(2)}) copy-start(pred[16,2048]{1,0:T(8,128)(4,1)S(1)} %get-tuple-element.18) | copy-start | bytes 98308
  9.2 119.0 %copy-start.23 = (pred[16,2048]{1,0:T(8,128)(4,1)}, pred[16,2048]{1,0:T(8,128)(4,1)S(1)}, u32[]{:S(2)}) copy-start(pred[16,2048]{1,0:T(8,128)(4,1)S(1)} %get-tuple-element.19) | copy-start | bytes 98308
  9.2 119.0 %copy-start.25 = (pred[16,2048]{1,0:T(8,128)(4,1)}, pred[16,2048]{1,0:T(8,128)(4,1)S(1)}, u32[]{:S(2)}) copy-start(pred[16,2048]{1,0:T(8,128)(4,1)S(1)} %get-tuple-element.20) | copy-start | bytes 98308
  9.2 119.0 %copy-start.27 = (pred[16,2048]{1,0:T(8,128)(4,1)}, pred[16,2048]{1,0:T(8,128)(4,1)S(1)}, u32[]{:S(2)}) copy-start(pred[16,2048]{1,0:T(8,128)(4,1)S(1)} %get-tuple-element.21) | copy-start | bytes 98308
  9.2 119.0 %copy-start.29 = (pred[16,2048]{1,0:T(8,128)(4,1)}, pred[16,2048]{1,0:T(8,128)(4,1)S(1)}, u32[]{:S(2)}) copy-start(pred[16,2048]{1,0:T(8,128)(4,1)S(1)} %get-tuple-element.22) | copy-start | bytes 98308
  9.2 119.0 %copy-start.31 = (pred[16,2048]{1,0:T(8,128)(4,1)}, pred[16,2048]{1,0:T(8,128)(4,1)S(1)}, u32[]{:S(2)}) copy-start(pred[16,2048]{1,0:T(8,128)(4,1)S(1)} %get-tuple-element.23) | copy-start | bytes 98308
  9.2 119.0 %copy-start.33 = (pred[16,2048]{1,0:T(8,128)(4,1)}, pred[16,2048]{1,0:T(8,128)(4,1)S(1)}, u32[]{:S(2)}) copy-start(pred[16,2048]{1,0:T(8,128)(4,1)S(1)} %get-tuple-element.24) | copy-start | bytes 98308
  15.0 113.2 %copy-start.6 = (s32[16,2048]{1,0:T(8,128)}, s32[16,2048]{1,0:T(8,128)S(1)}, u32[]{:S(2)}) copy-start(s32[16,2048]{1,0:T(8,128)S(1)} %get-tuple-element.26) | copy-start | bytes 393220
  15.1 113.1 %copy-start.8 = (s32[16,2048]{1,0:T(8,128)}, s32[16,2048]{1,0:T(8,128)S(1)}, u32[]{:S(2)}) copy-start(s32[16,2048]{1,0:T(8,128)S(1)} %get-tuple-element.27) | copy-start | bytes 393220
  15.2 113.1 %copy-start.10 = (s32[16,2048]{1,0:T(8,128)}, s32[16,2048]{1,0:T(8,128)S(1)}, u32[]{:S(2)}) copy-start(s32[16,2048]{1,0:T(8,128)S(1)} %get-tuple-element.28) | copy-start | bytes 393220
  15.3 113.0 %copy-start.12 = (s32[16,2048]{1,0:T(8,128)}, s32[16,2048]{1,0:T(8,128)S(1)}, u32[]{:S(2)}) copy-start(s32[16,2048]{1,0:T(8,128)S(1)} %get-tuple-element.29) | copy-start | bytes 393220
  15.3 113.0 %copy-start.14 = (s32[16,2048]{1,0:T(8,128)}, s32[16,2048]{1,0:T(8,128)S(1)}, u32[]{:S(2)}) copy-start(s32[16,2048]{1,0:T(8,128)S(1)} %get-tuple-element.30) | copy-start | bytes 393220
  134.9 233.1 %all-to-all-start = ((bf16[16,16,128,256]{3,2,0,1:T(8,128)(2,1)}), bf16[16,16,128,256]{3,2,0,1:T(8,128)(2,1)}, u32[]{:S(2)}, u32[]{:S(2)}) async-start(bf16[16,16,128,256]{3,2,0,1:T(8,128)(2,1)} %copy.44), calls=%async_computation | async-start | bytes 33554432 | tf_op jit(solution)/shard_map/all_to_all | solution.py:28
  143.0 718.7 %all-reduce.5.cloned.1.call-start = ((), (), s32[]{:S(2)}) async-start(), calls=%async_computation.3 | async-start | bytes 8388608 | tf_op jit(solution)/shard_map/psum | solution.py:66
  368.0 17.4 %copy-start.18 = (bf16[256,16]{0,1:T(8,128)(2,1)S(1)}, bf16[256,16]{0,1:T(8,128)(2,1)}, u32[]{:S(2)}) copy-start(bf16[256,16]{0,1:T(8,128)(2,1)} %param.10) | copy-start | bytes 24580
  605.8 12.2 copy-start.13
  605.8 12.2 copy-start.15
  605.9 12.2 copy-start.20
  605.9 12.2 copy-start.22
  605.9 12.2 copy-start.24
  605.9 12.2 copy-start.26
  605.9 12.2 copy-start.28
  605.9 12.2 copy-start.30
  605.9 12.2 copy-start.32
  605.9 12.2 copy-start.34
  618.1 107.9 %copy-start.4 = (bf16[4096,128]{0,1:T(8,128)(2,1)S(1)}, bf16[4096,128]{0,1:T(8,128)(2,1)}, u32[]{:S(2)}) copy-start(bf16[4096,128]{0,1:T(8,128)(2,1)} %copy-done.3) | copy-start | bytes 3145732
  618.1 107.9 %copy-start.17 = (bf16[8,8,128]{2,1,0:T(8,128)(2,1)S(1)}, bf16[8,8,128]{2,1,0:T(8,128)(2,1)}, u32[]{:S(2)}) copy-start(bf16[8,8,128]{2,1,0:T(8,128)(2,1)} %copy-done.16) | copy-start | bytes 49156
  618.1 110.5 %copy-start.5 = (bf16[4096,128]{0,1:T(8,128)(2,1)S(1)}, bf16[4096,128]{0,1:T(8,128)(2,1)}, u32[]{:S(2)}) copy-start(bf16[4096,128]{0,1:T(8,128)(2,1)} %get-tuple-element.8) | copy-start | bytes 3145732
  726.0 665.2 %reduce-scatter.2.cloned.1.call-start = ((), (), s32[]{:S(2)}) async-start(), calls=%async_computation.4 | async-start | bytes 2113536 | tf_op jit(solution)/shard_map/reduce_scatter | solution.py:68
  728.7 662.5 %copy-start.1 = (bf16[4096,64]{0,1:T(8,128)(2,1)S(1)}, bf16[4096,64]{0,1:T(8,128)(2,1)}, u32[]{:S(2)}) copy-start(bf16[4096,64]{0,1:T(8,128)(2,1)} %param.11) | copy-start | bytes 1572868
  (8 other events, 64.6 us)
Sparse Core Ops, SparseCore 0:
  726.1 103.6 all-reduce.4
Sparse Core Ops, SparseCore 1:
  729.4 661.8 reduce-scatter.1
where the time goes:
time: 1400 us
  waiting for transfers between devices  748 us (53%)
  blocking collectives  314 us (22%)
  matrix products  252 us (18%)
  local copies, waits for them, and re-layouts  53.7 us (4%)
  between operations  16.1 us (1%)
    reduce_scatter x1, waiting for transfers between devices, local(): lax.psum_scatter(hidden_part, ('replica', 'mp'), scatter_dimension=0, til...  523 us
    all_to_all x1, waiting for transfers between devices, local(): lax.all_to_all(outgoing, 'mp', split_axis=1, concat_axis=0, tiled=True)  225 us
    all_to_all x1, blocking collectives, local(): lax.all_to_all(d_pooled.reshape(model_size, fields_here, local_rows, emb_...  193 us
    unnamed x1, blocking collectives  121 us
    dot_general x1, matrix products, local(): jnp.einsum('frb,fre->fbe', counts, tables, preferred_element_type=jnp.flo...  113 us
    dot_general x1, matrix products, local(): jnp.einsum('frb,fbe->fre', counts, d_rows, preferred_element_type=jnp.flo...  108 us
  transfers between devices with their start and end apart: 3, of which 2 were waited for; matrix products, arithmetic and copies ran while one was open for 2% of the time, Pallas kernels for 0%

commit v1 on v0

v1 whole, which is shorter than its diff:
```python
import functools

import jax
import jax.numpy as jnp
from jax import lax
from jax.experimental import pallas as pl
from jax.experimental.pallas import tpu as pltpu
from jax.sharding import PartitionSpec as P

MESH = pl.DeviceIdType.MESH
K1 = 8
K2 = 8
KK = K1 + K2
SUB = 16
HI = 64
BITS = 4
VMEM = 60 * 1024 * 1024
F32 = jnp.float32
BF16 = jnp.bfloat16


def peers():
    me = lax.axis_index("mp")
    core = lax.rem(me, 2)
    y = lax.rem(lax.div(me, 2), 4)
    z = lax.div(me, 8)
    other = me + 1 - 2 * core
    right = z * 8 + lax.rem(y + 1, 4) * 2 + core
    left = z * 8 + lax.rem(y + 3, 4) * 2 + core
    across = (1 - z) * 8 + y * 2 + core
    return me, core, y, z, other, right, left, across


def barrier(devices):
    sem = pltpu.get_barrier_semaphore()
    for d in devices:
        pl.semaphore_signal(sem, inc=1, device_id={"mp": d}, device_id_type=MESH)
    pl.semaphore_wait(sem, len(devices))


def remote(src, dst, send, recv, device):
    return pltpu.make_async_remote_copy(
        src_ref=src, dst_ref=dst, send_sem=send, recv_sem=recv, device_id={"mp": device}, device_id_type=MESH
    )


def digits(words):
    return jnp.concatenate(
        [(lax.shift_right_logical(words, BITS * d) & 15).astype(F32).astype(BF16) for d in range(8)], axis=0
    )


def fwd_kernel(
    idx, lens, tab_t, kron, words_out, pooled_out, fac_out,
    sbuf, rcore, rhalf, rfull, rz, wbuf, pbuf,
    core_s, core_r, half_s, half_r, full_s, full_r, z_s, z_r, w_sem, p_sem,
):
    me, core, y, z, other, right, left, across = peers()
    barrier((other, right, left, across))
    n_f = idx.shape[0]
    emb = tab_t.shape[1]

    def zo_of(t):
        return jnp.where(t < 2, t, jnp.where(t < 6, lax.div(t - 2, 2), t - 6))

    def chunk_of(t):
        dy = jnp.where(t < 2, 2, jnp.where(t < 6, 1 + 2 * lax.rem(t, 2), 0))
        zo = zo_of(t)
        zt = lax.rem(z + 1 + zo, 2)
        return zt * 4 + lax.rem(y + dy, 4)

    def p_copy(t):
        slot = lax.rem(t, 2)
        return pltpu.make_async_copy(pbuf.at[slot], pooled_out.at[chunk_of(t)], p_sem.at[slot])

    def w_copy(t):
        return pltpu.make_async_copy(wbuf.at[t], words_out.at[chunk_of(t)], w_sem.at[t])

    def core_copy(t):
        return remote(sbuf.at[t, 1 - core], rcore.at[t], core_s.at[t], core_r.at[t], other)

    def half_copy(t, zo, d):
        return remote(
            sbuf.at[t, core, pl.ds(d * K1, K1)], rhalf.at[zo, d], half_s.at[zo, d], half_r.at[zo, d], (right, left)[d]
        )

    def full_copy(t, zo, d):
        return remote(sbuf.at[t, core], rfull.at[zo, d], full_s.at[zo, d], full_r.at[zo, d], (right, left)[d])

    def z_copy():
        return remote(sbuf.at[6, core], rz, z_s, z_r, across)

    def compute(t):
        q = chunk_of(t)
        slot = lax.rem(t, 2)
        where = pl.ds(pl.multiple_of(q * 256, 256), 256)

        @pl.when(t >= 2)
        def _():
            p_copy(t - 2).wait()

        def field(f, carry):
            ids = idx[f, :, where]
            live = lens[pl.ds(f, 1), where]
            lane_slot = lax.broadcasted_iota(jnp.int32, ids.shape, 0)
            hi = ids & (HI - 1)
            val = jnp.where(lane_slot < live, jnp.left_shift(1, BITS * lax.shift_right_logical(ids, 6)), 0)
            rows = lax.broadcasted_iota(jnp.int32, (HI, 256), 0)
            words = jnp.zeros((HI, 256), jnp.int32)
            for s in range(8):
                words = words + jnp.where(hi[s : s + 1, :] == rows, val[s : s + 1, :], 0)
            wbuf[t, f] = words
            pooled = jnp.dot(tab_t[f], digits(words), preferred_element_type=F32)
            pbuf[slot, f] = pooled.astype(BF16)
            return carry

        lax.fori_loop(0, n_f, field, 0)
        p_copy(t).start()
        w_copy(t).start()

        def block(eb, carry):
            rows = pl.ds(pl.multiple_of(eb * SUB, SUB), SUB)
            x = pbuf[slot, :, rows, :].reshape(n_f * SUB, 256)
            part = jnp.dot(kron[...], x, preferred_element_type=F32).astype(BF16).reshape(KK, SUB, 256)
            sbuf[t, 0, :, rows, :] = part[:, :, :128]
            sbuf[t, 1, :, rows, :] = part[:, :, 128:]
            return carry

        lax.fori_loop(0, emb // SUB, block, 0)
        core_copy(t).start()

    def add(t, pairs, out=None):
        def one(k, carry, refs):
            total = sbuf[t, core, k].astype(F32)
            for r, first in refs:
                total = total + r[k - first].astype(F32)
            if out is None:
                sbuf[t, core, k] = total.astype(BF16)
            else:
                out[k] = total
            return carry

        lax.fori_loop(0, K1, functools.partial(one, refs=[(r, a) for r, a, b in pairs if a < K1]), 0)
        lax.fori_loop(K1, KK, functools.partial(one, refs=[(r, a) for r, a, b in pairs if b > K1]), 0)

    def pass_on(t):
        core_copy(t).wait_recv()
        mine = (rcore.at[t], 0, KK)

        @pl.when(t < 2)
        def _():
            add(t, [mine])
            half_copy(t, zo_of(t), 0).start()
            half_copy(t, zo_of(t), 1).start()

        for d in range(2):

            @pl.when(jnp.logical_or(t == 2 + d, t == 4 + d))
            def _():
                zo = zo_of(t)
                half_copy(zo, zo, d).wait_recv()
                add(t, [mine, (rhalf.at[zo, d], d * K1, d * K1 + K1)])
                full_copy(t, zo, d).start()

        @pl.when(t == 6)
        def _():
            for d in range(2):
                full_copy(2 + d, 0, d).wait_recv()
            add(t, [mine, (rfull.at[0, 0], 0, KK), (rfull.at[0, 1], 0, KK)])
            z_copy().start()

    def step(t, carry):
        compute(t)

        @pl.when(t >= 1)
        def _():
            pass_on(t - 1)

        return carry

    lax.fori_loop(0, 8, step, 0)
    core_copy(7).wait_recv()
    for d in range(2):
        full_copy(4 + d, 1, d).wait_recv()
    z_copy().wait_recv()
    add(
        7, [(rcore.at[7], 0, KK), (rfull.at[1, 0], 0, KK), (rfull.at[1, 1], 0, KK), (rz, 0, KK)], fac_out
    )

    for t in range(8):
        core_copy(t).wait_send()
        w_copy(t).wait()
    for zo in range(2):
        for d in range(2):
            half_copy(zo, zo, d).wait_send()
            full_copy(2 + 2 * zo + d, zo, d).wait_send()
    z_copy().wait_send()
    p_copy(6).wait()
    p_copy(7).wait()


def forward(indices, lengths, tab_t, kron):
    n_f, emb, _ = tab_t.shape
    dma = pltpu.SemaphoreType.DMA
    vmem = pl.BlockSpec(memory_space=pltpu.VMEM)
    hbm = pl.BlockSpec(memory_space=pl.ANY)
    return pl.pallas_call(
        fwd_kernel,
        out_shape=(
            jax.ShapeDtypeStruct((8, n_f, HI, 256), jnp.int32),
            jax.ShapeDtypeStruct((8, n_f, emb, 256), BF16),
            jax.ShapeDtypeStruct((KK, emb, 128), F32),
        ),
        in_specs=[vmem] * 4,
        out_specs=(hbm, hbm, vmem),
        scratch_shapes=[
            pltpu.VMEM((8, 2, KK, emb, 128), BF16),
            pltpu.VMEM((8, KK, emb, 128), BF16),
            pltpu.VMEM((2, 2, K1, emb, 128), BF16),
            pltpu.VMEM((2, 2, KK, emb, 128), BF16),
            pltpu.VMEM((KK, emb, 128), BF16),
            pltpu.VMEM((8, n_f, HI, 256), jnp.int32),
            pltpu.VMEM((2, n_f, emb, 256), BF16),
            dma((8,)), dma((8,)), dma((2, 2)), dma((2, 2)), dma((2, 2)), dma((2, 2)), dma, dma, dma((8,)), dma((2,)),
        ],
        compiler_params=pltpu.CompilerParams(collective_id=0, has_side_effects=True, vmem_limit_bytes=VMEM),
        cost_estimate=pl.CostEstimate(flops=15 * 10**9, bytes_accessed=40 * 10**6, transcendentals=0),
    )(indices, lengths, tab_t, kron)


def nt(a, b):
    return lax.dot_general(a, b, (((1,), (1,)), ((), ())), preferred_element_type=F32)


def dense_kernel(fac, wh, wh_t, wo_col, wo_row, dl, logits, outp, hidp, dfac, inter):
    hid, _ = wh.shape
    emb = fac.shape[1]
    step = 512

    def left(i, carry):
        a = fac[i]
        for j in range(K2):
            inter[pl.ds(i * K2 + j, 1), :] = jnp.sum(a * fac[K1 + j], axis=0, keepdims=True)
        return carry

    lax.fori_loop(0, K1, left, 0)
    feat = inter[...].astype(BF16)
    row = dl[...]
    d0 = row.astype(BF16)
    r1 = row - d0.astype(F32)
    d1 = r1.astype(BF16)
    d2 = (r1 - d1.astype(F32)).astype(BF16)
    sub = lax.broadcasted_iota(jnp.int32, (8, row.shape[1]), 0)
    d_rows = jnp.where(
        sub == 0, d0.astype(F32), jnp.where(sub == 1, d1.astype(F32), jnp.where(sub == 2, d2.astype(F32), 0.0))
    ).astype(BF16)
    wo8 = wo_row[...]

    def top(c, carry):
        logit_acc, d_inter = carry
        at = pl.ds(pl.multiple_of(c * step, step), step)
        v = jnp.dot(wh[at, :], feat, preferred_element_type=F32)
        s = jax.nn.sigmoid(v)
        hidden = (v * s).astype(BF16)
        logit_acc = logit_acc + jnp.dot(wo_row[:, at], hidden, preferred_element_type=F32)
        outp[:, at] = nt(d_rows, hidden)
        d_hidden = (wo_col[at, :].astype(F32) * row * s * (1.0 + v * (1.0 - s))).astype(BF16)
        hidp[at, :] = nt(d_hidden, feat)
        d_inter = d_inter + jnp.dot(wh_t[:, at], d_hidden, preferred_element_type=F32)
        return logit_acc, d_inter

    del wo8
    n = row.shape[1]
    logit_acc, d_inter = lax.fori_loop(
        0, hid // step, top, (jnp.zeros((8, n), F32), jnp.zeros((K1 * K2, n), F32))
    )
    logits[...] = logit_acc[0:1]
    inter[...] = d_inter

    def back(eb, carry):
        rows = pl.ds(pl.multiple_of(eb * SUB, SUB), SUB)
        right = [fac[K1 + j, rows, :] for j in range(K2)]
        d_right = [jnp.zeros((SUB, n), F32) for _ in range(K2)]
        for i in range(K1):
            a = fac[i, rows, :]
            d_left = jnp.zeros((SUB, n), F32)
            for j in range(K2):
                g = inter[pl.ds(i * K2 + j, 1), :]
                d_left = d_left + g * right[j]
                d_right[j] = d_right[j] + g * a
            dfac[i, rows, :] = d_left.astype(BF16)
        for j in range(K2):
            dfac[K1 + j, rows, :] = d_right[j].astype(BF16)
        return carry

    lax.fori_loop(0, emb // SUB, back, 0)


def dense(fac, w_hidden, w_out, d_logit):
    hid, feat = w_hidden.shape
    n = d_logit.shape[0]
    wo_row = jnp.broadcast_to(w_out[None, :], (8, hid))
    return pl.pallas_call(
        dense_kernel,
        out_shape=(
            jax.ShapeDtypeStruct((1, n), F32),
            jax.ShapeDtypeStruct((8, hid), F32),
            jax.ShapeDtypeStruct((hid, feat), F32),
            jax.ShapeDtypeStruct(fac.shape, BF16),
        ),
        scratch_shapes=[pltpu.VMEM((feat, n), F32)],
        compiler_params=pltpu.CompilerParams(vmem_limit_bytes=VMEM),
        cost_estimate=pl.CostEstimate(flops=10**9, bytes_accessed=10**7, transcendentals=10**6),
    )(fac, w_hidden, w_hidden.T, w_out[:, None], wo_row, d_logit[None, :])


def bwd_kernel(
    dfac, words, pooled, kron_t, tg_out, pg_out,
    gbuf, acc, dpool, wbuf, pbuf,
    own_sem, w_sem, p_sem, core_s, core_r, ici_s, ici_r, half_s, half_r,
):
    me, core, y, z, other, right, left, across = peers()
    barrier((other, right, left, across))
    n_f = wbuf.shape[1]
    emb = dfac.shape[1]
    places = ((0, 0), (0, 3), (0, 1), (1, 0), (1, 3), (1, 1), (0, 2), (1, 2))

    def chip(n):
        dz, dy = places[n]
        return lax.rem(z + dz, 2) * 4 + lax.rem(y + dy, 4)

    def block(n):
        return chip(n) * 2 + core

    def to_core(n):
        return remote(gbuf.at[block(n)], gbuf.at[block(n)], core_s.at[n], core_r.at[n], other)

    def from_core(n):
        j = chip(n) * 2 + 1 - core
        return remote(gbuf.at[j], gbuf.at[j], core_s.at[n], core_r.at[n], other)

    def whole(n, m, device):
        j = block(n)
        return remote(gbuf.at[j], gbuf.at[j], ici_s.at[m], ici_r.at[m], device)

    def arrived(m):
        j = block(m)
        remote(gbuf.at[j], gbuf.at[j], ici_s.at[m], ici_r.at[m], right).wait_recv()

    def half(n, m, d):
        j = block(n)
        part = pl.ds(d * K1, K1)
        i = (m - 6, d)
        return remote(gbuf.at[j, part], gbuf.at[j, part], half_s.at[i], half_r.at[i], (right, left)[d])

    def half_arrived(m, d):
        j = block(m)
        part = pl.ds(d * K1, K1)
        i = (m - 6, d)
        remote(gbuf.at[j, part], gbuf.at[j, part], half_s.at[i], half_r.at[i], right).wait_recv()

    def w_copy(n):
        return pltpu.make_async_copy(words.at[chip(n)], wbuf.at[n % 2], w_sem.at[n % 2])

    def p_copy(n):
        return pltpu.make_async_copy(pooled.at[chip(n)], pbuf.at[n % 2], p_sem.at[n % 2])

    w_copy(0).start()
    p_copy(0).start()
    own = pltpu.make_async_copy(dfac, gbuf.at[me], own_sem)
    own.start()
    own.wait()
    sends = [whole(0, 1, right), whole(0, 2, left), whole(0, 3, across), to_core(0)]
    for s in sends:
        s.start()

    pg_out[...] = jnp.zeros_like(pg_out)

    def work(n, first):
        w_copy(n).wait()
        p_copy(n).wait()
        if n + 1 < 8:
            w_copy(n + 1).start()
            p_copy(n + 1).start()
        slot = n % 2
        base = chip(n) * 2

        def spread(eb, carry):
            rows = pl.ds(pl.multiple_of(eb * SUB, SUB), SUB)
            g = jnp.concatenate(
                [gbuf[base, :, rows, :].reshape(KK * SUB, 128), gbuf[base + 1, :, rows, :].reshape(KK * SUB, 128)],
                axis=1,
            )
            d = jnp.dot(kron_t[...], g, preferred_element_type=F32).astype(BF16)
            dpool[:, rows, :] = d.reshape(n_f, SUB, 256)
            x = pbuf[slot, :, rows, :].reshape(n_f * SUB, 256)
            pg_out[...] += nt(x, g)
            return carry

        lax.fori_loop(0, emb // SUB, spread, 0)

        def field(f, carry):
            part = nt(digits(wbuf[slot, f]), dpool[f])
            if first:
                acc[f] = part
            elif n == 7:
                tg_out[f] = (acc[f] + part).astype(BF16)
            else:
                acc[f] += part
            return carry

        lax.fori_loop(0, n_f, field, 0)

    def go(copy):
        copy.start()
        sends.append(copy)

    from_core(0).wait_recv()
    work(0, True)
    arrived(1)
    go(half(1, 6, 0))
    go(to_core(1))
    arrived(2)
    go(half(2, 6, 1))
    go(to_core(2))
    arrived(3)
    go(whole(3, 4, right))
    go(whole(3, 5, left))
    go(to_core(3))
    from_core(1).wait_recv()
    work(1, False)
    from_core(2).wait_recv()
    work(2, False)
    for d in range(2):
        half_arrived(6, d)
    go(to_core(6))
    from_core(3).wait_recv()
    work(3, False)
    arrived(4)
    go(half(4, 7, 0))
    go(to_core(4))
    arrived(5)
    go(half(5, 7, 1))
    go(to_core(5))
    from_core(4).wait_recv()
    work(4, False)
    from_core(5).wait_recv()
    work(5, False)
    from_core(6).wait_recv()
    work(6, False)
    for d in range(2):
        half_arrived(7, d)
    go(to_core(7))
    from_core(7).wait_recv()
    work(7, False)
    for s in sends:
        s.wait_send()


def backward(dfac, words, pooled, kron_t):
    _, n_f, emb, _ = pooled.shape
    rows = 8 * HI
    dma = pltpu.SemaphoreType.DMA
    vmem = pl.BlockSpec(memory_space=pltpu.VMEM)
    hbm = pl.BlockSpec(memory_space=pl.ANY)
    return pl.pallas_call(
        bwd_kernel,
        out_shape=(
            jax.ShapeDtypeStruct((n_f, rows, emb), BF16),
            jax.ShapeDtypeStruct((n_f * SUB, KK * SUB), F32),
        ),
        in_specs=[vmem, hbm, hbm, vmem],
        out_specs=(vmem, vmem),
        scratch_shapes=[
            pltpu.VMEM((16,) + dfac.shape, BF16),
            pltpu.VMEM((n_f, rows, emb), F32),
            pltpu.VMEM((n_f, emb, 256), BF16),
            pltpu.VMEM((2, n_f, HI, 256), jnp.int32),
            pltpu.VMEM((2, n_f, emb, 256), BF16),
            dma, dma((2,)), dma((2,)), dma((8,)), dma((8,)), dma((6,)), dma((6,)), dma((2, 2)), dma((2, 2)),
        ],
        compiler_params=pltpu.CompilerParams(collective_id=1, has_side_effects=True, vmem_limit_bytes=VMEM),
        cost_estimate=pl.CostEstimate(flops=20 * 10**9, bytes_accessed=40 * 10**6, transcendentals=0),
    )(dfac, words, pooled, kron_t)


def scatter_sum(x):
    rows = x.shape[0] // 128
    x = x.reshape(8, 16, rows, x.shape[1])
    x = lax.all_to_all(x, "mp", 1, 1, tiled=True).sum(1)
    return lax.all_to_all(x, "replica", 0, 0, tiled=True).sum(0)


def local(indices, lengths, tables, proj, w_hidden, w_out, d_logit):
    n_f = indices.shape[0]
    me = lax.axis_index("mp")
    here = lax.dynamic_slice_in_dim(proj, me * n_f, n_f, 0)
    eye = jnp.eye(SUB, dtype=BF16)
    kron_t = (here[:, None, :, None] * eye[None, :, None, :]).reshape(n_f * SUB, KK * SUB)
    words, pooled, fac = forward(indices, lengths, tables.transpose(0, 2, 1), kron_t.T)
    logits, out_part, hidden_part, dfac = dense(fac, w_hidden, w_out, d_logit)
    table_part, pg = backward(dfac, words, pooled, kron_t)
    table_grad = lax.psum(table_part, "replica").astype(F32)
    pg = jnp.einsum("fakb,ab->fk", pg.reshape(n_f, SUB, KK, SUB), jnp.eye(SUB, dtype=F32), precision="highest")
    pg_all = lax.dynamic_update_slice_in_dim(jnp.zeros(proj.shape, F32), pg, me * n_f, 0)
    place = lax.axis_index("replica") * 16 + me
    pg_all = lax.psum(pg_all, ("replica", "mp"))
    proj_share = lax.dynamic_slice_in_dim(pg_all, place * (proj.shape[0] // 128), proj.shape[0] // 128, 0)
    both = jnp.concatenate([hidden_part, out_part.sum(0)[:, None]], axis=1)
    both = scatter_sum(both)
    return (logits.reshape(-1), table_grad, both[:, :-1], both[:, -1], proj_share)


def solution(mesh):
    in_specs = (
        P("mp", None, "replica"),
        P("mp", "replica"),
        P("mp", None, None),
        P(),
        P(),
        P(),
        P(("replica", "mp")),
    )
    out_specs = (
        P(("replica", "mp")),
        P("mp", None, None),
        P(("replica", "mp"), None),
        P(("replica", "mp")),
        P(("replica", "mp"), None),
    )
    return jax.shard_map(local, mesh=mesh, in_specs=in_specs, out_specs=out_specs, check_vma=False)
```

time: 1400 us -> 413 us (0.29)
  waiting for transfers between devices: 748 us -> 6.04 us
  matrix products: 252 us -> 5.34 us
  Pallas kernels: 0 us -> 214 us
  blocking collectives: 314 us -> 133 us
  local copies, waits for them, and re-layouts: 53.7 us -> 17.6 us
    reduce_scatter x1 -> x0, waiting for transfers between devices: 523 us -> none  [local(): lax.psum_scatter(hidden_part, ('replica', 'mp'), scatter_dimension=0, til...]
    dot_general x13 -> x1, matrix products: 252 us -> 5.34 us  [local(): jnp.einsum('fakb,ab->fk', pg.reshape(n_f, SUB, KK, SUB), jnp.eye(SUB, dty...]
    all_to_all x1 -> x2, waiting for transfers between devices: 225 us -> 6.02 us  [the longest x1 6.02 us: scatter_sum(): return lax.all_to_all(x, 'replica', 0, 0, tiled=True).sum(0)]
    pallas_call x0 -> x3, Pallas kernels: none -> 214 us  [the longest x1 103 us: forward(): pl.pallas_call(fwd_kernel, out_shape=(jax.ShapeDtypeStruct((8, n_f, HI, 2...]
    all_to_all x1 -> x0, blocking collectives: 193 us -> none  [local(): lax.all_to_all(d_pooled.reshape(model_size, fields_here, local_rows, emb_...]
    psum x0 -> x1, blocking collectives: none -> 133 us  [local(): pg_all = lax.psum(pg_all, ('replica', 'mp'))]
    unnamed x1 -> x0, blocking collectives: 121 us -> none
    all_to_all x2 -> x0, local copies, waits for them, and re-layouts: 23.7 us -> none  [the longest x1 12.1 us: local(): lax.all_to_all(d_pooled.reshape(model_size, fields_here, local_rows, emb_...]
  transfers between devices with their start and end apart: 3 -> 3, of which waited for: 2 -> 1; matrix products, arithmetic and copies ran while one was open for 2% -> 3% of each run, Pallas kernels for 0% -> 0%
where the time goes in v1:
time: 413 us; the launch traced here: 412 us
  Pallas kernels  214 us (52%)
  blocking collectives  133 us (32%)
  local copies, waits for them, and re-layouts  17.6 us (4%)
  between operations  14.2 us (3%)
  other arithmetic  11.2 us (3%)
  starting transfers between devices  10.4 us (3%)
  waiting for transfers between devices  6.04 us (1%)
  matrix products  5.34 us (1%)
    psum x1, blocking collectives, local(): pg_all = lax.psum(pg_all, ('replica', 'mp'))  133 us
    pallas_call x1, Pallas kernels, forward(): pl.pallas_call(fwd_kernel, out_shape=(jax.ShapeDtypeStruct((8, n_f, HI, 2...  103 us
    pallas_call x1, Pallas kernels, backward(): pl.pallas_call(bwd_kernel, out_shape=(jax.ShapeDtypeStruct((n_f, rows, em...  101 us
    pallas_call x1, Pallas kernels, dense(): pl.pallas_call(dense_kernel, out_shape=(jax.ShapeDtypeStruct((1, n), F32)...  9.9 us
    unnamed x18, local copies, waits for them, and re-layouts  9.31 us
  transfers between devices with their start and end apart: 3, of which 1 were waited for; matrix products, arithmetic and copies ran while one was open for 3% of the time, Pallas kernels for 0%

profile of v1, /device:TPU:0, one launch (start us, length us, event | category | flops | bytes accessed | tf_op | source)
XLA Modules:
  0.0 412.1 jit_solution(16882650214055272615)
XLA Ops:
  7.2 0.0 copy-start
  7.2 0.0 all-reduce.2.cloned.1.call-start
  7.2 0.6 copy-done
  7.9 0.1 constant_dynamic-slice_fusion.1
  7.9 0.1 copy.30
  8.0 0.1 broadcast_multiply_fusion
  8.2 1.0 mul.31.kron_t
  9.2 0.8 copy.31.kron
  10.0 6.5 %copy.29 = bf16[16,512,256]{1,2,0:T(8,128)(2,1)} copy(bf16[16,512,256]{2,1,0:T(8,128)(2,1)} %param.9) | data formatting | bytes 8388608 | tf_op args[2]
  16.4 1.6 broadcast_in_dim.22.wo_col
  18.0 1.3 copy.32.wh
  19.3 103.3 %shard_map.110 = (s32[8,16,64,256]{3,2,1,0:T(8,128)}, bf16[8,16,256,256]{3,2,1,0:T(8,128)(2,1)}, f32[16,256,128]{2,1,0:T(8,128)}) custom-call(s32[16,8,2048]{2,1,0:T(8,128)} %idx.1, s32[16,2048]{1,0:T(8,128)} %lens.1, bf16[16,256,512]{2,1,0:T(8,128)(2,1)} %bitcast.15, bf16[256,256]{1,0:T(8,128)(2,1)} %copy.31.kron), custom_call_target="tpu_custom_call" | custom-call | flops 15000000512 | bytes 40000000 | tf_op jit(solution)/shard_map/pallas_call | solution.py:207
  122.7 0.6 broadcast_in_dim.9.wo_row
  123.3 9.9 %shard_map.111 = (f32[1,128]{1,0:T(1,128)}, f32[8,4096]{1,0:T(8,128)}, f32[4096,64]{1,0:T(8,128)}, bf16[16,256,128]{2,1,0:T(8,128)(2,1)}) custom-call(f32[16,256,128]{2,1,0:T(8,128)} %get-tuple-element.14.fac, bf16[4096,64]{1,0:T(8,128)(2,1)} %copy.32.wh, bf16[64,4096]{1,0:T(8,128)(2,1)} %bitcast.17, bf16[4096,1]{1,0:T(8,128)(2,1)} %broadcast_in_dim.22.wo_col, ...), custom_call_target="tpu_custom_call" | custom-call | flops 1000000000 | bytes 10000000 | tf_op jit(solution)/shard_map/pallas_call | solution.py:303
  133.2 101.1 %shard_map.112 = (bf16[16,512,256]{2,1,0:T(8,128)(2,1)}, f32[256,256]{1,0:T(8,128)}) custom-call(bf16[16,256,128]{2,1,0:T(8,128)(2,1)} %get-tuple-element.16.dfac, s32[8,16,64,256]{3,2,1,0:T(8,128)} %get-tuple-element.17.words, bf16[8,16,256,256]{3,2,1,0:T(8,128)(2,1)} %get-tuple-element.18.pooled, bf16[256,256]{1,0:T(8,128)(2,1)} %copy-done.3), custom_call_target="tpu_custom_call" | custom-call | flops 20000000000 | bytes 40000000 | tf_op jit(solution)/shard_map/pallas_call | solution.py:466
  234.3 0.0 all-reduce.2.cloned.1.call-update
  234.4 0.9 copy-done.5
  235.3 0.1 concatenate.9
  235.3 0.8 copy.35
  236.2 3.6 pad_maximum_fusion
  239.8 5.5 %all-to-all-start = ((f32[8,16,32,65]{3,2,0,1:T(8,128)}), f32[8,16,32,65]{3,2,0,1:T(8,128)S(1)}, u32[]{:S(2)}, u32[]{:S(2)}) async-start(f32[8,16,32,65]{3,2,0,1:T(8,128)} %pad_maximum_fusion), calls=%async_computation | async-start | bytes 4194304 | tf_op jit(solution)/shard_map/all_to_all | solution.py:490
  245.3 2.0 reshape.35
  247.3 5.3 %fusion = f32[1,16,16,1]{2,0,3,1:T(1,128)S(1)} fusion(f32[16,16,16,16]{3,2,1,0:T(8,128)} %reshape.35, pred[16,16,1,1]{1,0,2,3:T(8,128)(4,1)S(1)} %fusion.2), kind=kOutput, calls=%fused_computation.2 | convolution fusion | flops 786432 | bytes 263424 | tf_op jit(solution)/shard_map/fakb,ab->fk/dot_general | solution.py:504
  252.7 132.9 %psum.15 = f32[256,16]{1,0:T(8,128)S(1)} all-reduce(f32[256,16]{1,0:T(8,128)S(1)} %constant_dynamic-update-slice_fusion), channel_id=1, replica_groups=mesh['replica'=8,'mp'=16] {'replica','mp'}, use_global_device_ids=true, to_apply=%region_4.0 | all-reduce | flops 4096 | bytes 32768 | tf_op jit(solution)/shard_map/psum | solution.py:507
  385.6 0.0 all-to-all-done
  385.7 0.9 reduce_sum.28
  386.6 4.8 %all-to-all-start.1 = ((f32[8,32,65]{2,1,0:T(8,128)}), f32[8,32,65]{2,1,0:T(8,128)S(1)}, u32[]{:S(2)}, u32[]{:S(2)}) async-start(f32[8,32,65]{2,1,0:T(8,128)} %reduce_sum.28), calls=%async_computation.1 | async-start | bytes 262144 | tf_op jit(solution)/shard_map/all_to_all | solution.py:491
  391.4 0.6 constant_dynamic-slice_fusion
  391.9 6.0 %all-to-all-done.1 = f32[8,32,65]{2,1,0:T(8,128)S(1)} async-done(((f32[8,32,65]{2,1,0:T(8,128)}), f32[8,32,65]{2,1,0:T(8,128)S(1)}, u32[]{:S(2)}, u32[]{:S(2)}) %all-to-all-start.1) | async-done | bytes 66592 | tf_op jit(solution)/shard_map/all_to_all | solution.py:491
  398.0 0.0 copy-start.6
  398.0 0.7 slice_reduce_fusion
  398.7 6.5 %convert_element_type.12 = f32[16,512,256]{2,1,0:T(8,128)} convert(bf16[16,512,256]{2,1,0:T(8,128)(2,1)} %all-reduce.2.cloned.1.call-done) | non-fusion elementwise | flops 2097152 | bytes 12582912 | tf_op jit(solution)/shard_map/convert_element_type | solution.py:503
  (19 shorter events, 0.1 us)
Async XLA Ops:
  7.2 0.7 copy-start
  7.2 391.5 %all-reduce.2.cloned.1.call-start = ((), (), s32[]{:S(2)}) async-start(), calls=%async_computation.2 | async-start | bytes 8388608 | tf_op jit(solution)/shard_map/psum | solution.py:503
  9.2 7.3 %copy-start.3 = (bf16[256,256]{1,0:T(8,128)(2,1)}, bf16[256,256]{1,0:T(8,128)(2,1)S(1)}, u32[]{:S(2)}) copy-start(bf16[256,256]{1,0:T(8,128)(2,1)S(1)} %mul.31.kron_t) | copy-start | bytes 393220
  10.0 6.5 %copy-start.7 = (bf16[4096]{0:T(1024)(128)(2,1)S(1)}, bf16[4096]{0:T(1024)(128)(2,1)}, u32[]{:S(2)}) copy-start(bf16[4096]{0:T(1024)(128)(2,1)} %param.12) | copy-start | bytes 24580
  10.0 8.1 %copy-start.2 = (bf16[4096,64]{0,1:T(8,128)(2,1)S(1)}, bf16[4096,64]{0,1:T(8,128)(2,1)}, u32[]{:S(2)}) copy-start(bf16[4096,64]{0,1:T(8,128)(2,1)} %param.11) | copy-start | bytes 1572868
  234.3 0.9 copy-start.5
  239.8 5.6 %copy-start.4 = (f32[256,256]{1,0:T(8,128)S(1)}, f32[256,256]{1,0:T(8,128)}, u32[]{:S(2)}) copy-start(f32[256,256]{1,0:T(8,128)} %get-tuple-element.22) | copy-start | bytes 786436
  239.8 145.9 %all-to-all-start = ((f32[8,16,32,65]{3,2,0,1:T(8,128)}), f32[8,16,32,65]{3,2,0,1:T(8,128)S(1)}, u32[]{:S(2)}, u32[]{:S(2)}) async-start(f32[8,16,32,65]{3,2,0,1:T(8,128)} %pad_maximum_fusion), calls=%async_computation | async-start | bytes 4194304 | tf_op jit(solution)/shard_map/all_to_all | solution.py:490
  386.6 11.4 %all-to-all-start.1 = ((f32[8,32,65]{2,1,0:T(8,128)}), f32[8,32,65]{2,1,0:T(8,128)S(1)}, u32[]{:S(2)}, u32[]{:S(2)}) async-start(f32[8,32,65]{2,1,0:T(8,128)} %reduce_sum.28), calls=%async_computation.1 | async-start | bytes 262144 | tf_op jit(solution)/shard_map/all_to_all | solution.py:491
  398.0 7.2 %copy-start.6 = (f32[32,65]{1,0:T(8,128)}, f32[32,65]{1,0:T(8,128)S(1)}, u32[]{:S(2)}) copy-start(f32[32,65]{1,0:T(8,128)S(1)} %reduce_sum.29) | copy-start | bytes 24964
  398.7 6.5 %copy-start.1 = (bf16[256,16]{0,1:T(8,128)(2,1)S(1)}, bf16[256,16]{0,1:T(8,128)(2,1)}, u32[]{:S(2)}) copy-start(bf16[256,16]{0,1:T(8,128)(2,1)} %param.10) | copy-start | bytes 24580
Sparse Core Ops, SparseCore 0:
  234.5 122.4 all-reduce.1

commit v2 on v1

--- a/solution.py
+++ b/solution.py
@@ -24,23 +24,23 @@
     core = lax.rem(me, 2)
     y = lax.rem(lax.div(me, 2), 4)
     z = lax.div(me, 8)
-    other = me + 1 - 2 * core
-    right = z * 8 + lax.rem(y + 1, 4) * 2 + core
-    left = z * 8 + lax.rem(y + 3, 4) * 2 + core
-    across = (1 - z) * 8 + y * 2 + core
+    other = {"mp": me + 1 - 2 * core}
+    right = {"mp": z * 8 + lax.rem(y + 1, 4) * 2 + core}
+    left = {"mp": z * 8 + lax.rem(y + 3, 4) * 2 + core}
+    across = {"mp": (1 - z) * 8 + y * 2 + core}
     return me, core, y, z, other, right, left, across
 
 
 def barrier(devices):
     sem = pltpu.get_barrier_semaphore()
     for d in devices:
-        pl.semaphore_signal(sem, inc=1, device_id={"mp": d}, device_id_type=MESH)
+        pl.semaphore_signal(sem, inc=1, device_id=d, device_id_type=MESH)
     pl.semaphore_wait(sem, len(devices))
 
 
 def remote(src, dst, send, recv, device):
     return pltpu.make_async_remote_copy(
-        src_ref=src, dst_ref=dst, send_sem=send, recv_sem=recv, device_id={"mp": device}, device_id_type=MESH
+        src_ref=src, dst_ref=dst, send_sem=send, recv_sem=recv, device_id=device, device_id_type=MESH
     )
 
 
@@ -114,7 +114,7 @@
             pbuf[slot, f] = pooled.astype(BF16)
             return carry
 
-        lax.fori_loop(0, n_f, field, 0)
+        lax.fori_loop(0, n_f, field, 0, unroll=4)
         p_copy(t).start()
         w_copy(t).start()
 
@@ -126,7 +126,7 @@
             sbuf[t, 1, :, rows, :] = part[:, :, 128:]
             return carry
 
-        lax.fori_loop(0, emb // SUB, block, 0)
+        lax.fori_loop(0, emb // SUB, block, 0, unroll=4)
         core_copy(t).start()
 
     def add(t, pairs, out=None):
@@ -232,10 +232,10 @@
     return lax.dot_general(a, b, (((1,), (1,)), ((), ())), preferred_element_type=F32)
 
 
-def dense_kernel(fac, wh, wh_t, wo_col, wo_row, dl, logits, outp, hidp, dfac, inter):
-    hid, _ = wh.shape
+def dense_kernel(fac, wh, wh_t, wo_col, wo_row, dl, logits, grads, dfac, inter):
+    hid, n_feat = wh.shape
     emb = fac.shape[1]
-    step = 512
+    step = grads.shape[0] * grads.shape[2]
 
     def left(i, carry):
         a = fac[i]
@@ -246,15 +246,18 @@
     lax.fori_loop(0, K1, left, 0)
     feat = inter[...].astype(BF16)
     row = dl[...]
+    n = row.shape[1]
     d0 = row.astype(BF16)
     r1 = row - d0.astype(F32)
     d1 = r1.astype(BF16)
     d2 = (r1 - d1.astype(F32)).astype(BF16)
-    sub = lax.broadcasted_iota(jnp.int32, (8, row.shape[1]), 0)
+    sub = lax.broadcasted_iota(jnp.int32, (n_feat, n), 0)
     d_rows = jnp.where(
         sub == 0, d0.astype(F32), jnp.where(sub == 1, d1.astype(F32), jnp.where(sub == 2, d2.astype(F32), 0.0))
     ).astype(BF16)
-    wo8 = wo_row[...]
+    nil = jnp.zeros((n_feat, n), BF16)
+    feat_low = jnp.concatenate([feat, nil], axis=0)
+    d_high = jnp.concatenate([nil, d_rows], axis=0)
 
     def top(c, carry):
         logit_acc, d_inter = carry
@@ -263,22 +266,22 @@
         s = jax.nn.sigmoid(v)
         hidden = (v * s).astype(BF16)
         logit_acc = logit_acc + jnp.dot(wo_row[:, at], hidden, preferred_element_type=F32)
-        outp[:, at] = nt(d_rows, hidden)
         d_hidden = (wo_col[at, :].astype(F32) * row * s * (1.0 + v * (1.0 - s))).astype(BF16)
-        hidp[at, :] = nt(d_hidden, feat)
+        grad = nt(d_hidden, feat_low) + nt(hidden, d_high)
+        grads[:, pl.ds(c, 1), :, :] = grad.astype(BF16).reshape(grads.shape[0], 1, grads.shape[2], 2 * n_feat)
         d_inter = d_inter + jnp.dot(wh_t[:, at], d_hidden, preferred_element_type=F32)
         return logit_acc, d_inter
 
-    del wo8
-    n = row.shape[1]
     logit_acc, d_inter = lax.fori_loop(
-        0, hid // step, top, (jnp.zeros((8, n), F32), jnp.zeros((K1 * K2, n), F32))
+        0, hid // step, top, (jnp.zeros((8, n), F32), jnp.zeros((n_feat, n), F32))
     )
     logits[...] = logit_acc[0:1]
     inter[...] = d_inter
 
     def back(eb, carry):
+        p = lax.div(eb, emb // SUB // 2)
         rows = pl.ds(pl.multiple_of(eb * SUB, SUB), SUB)
+        low = pl.ds(pl.multiple_of(lax.rem(eb, emb // SUB // 2) * SUB, SUB), SUB)
         right = [fac[K1 + j, rows, :] for j in range(K2)]
         d_right = [jnp.zeros((SUB, n), F32) for _ in range(K2)]
         for i in range(K1):
@@ -288,9 +291,9 @@
                 g = inter[pl.ds(i * K2 + j, 1), :]
                 d_left = d_left + g * right[j]
                 d_right[j] = d_right[j] + g * a
-            dfac[i, rows, :] = d_left.astype(BF16)
+            dfac[p, i, low, :] = d_left.astype(BF16)
         for j in range(K2):
-            dfac[K1 + j, rows, :] = d_right[j].astype(BF16)
+            dfac[p, K1 + j, low, :] = d_right[j].astype(BF16)
         return carry
 
     lax.fori_loop(0, emb // SUB, back, 0)
@@ -304,9 +307,8 @@
         dense_kernel,
         out_shape=(
             jax.ShapeDtypeStruct((1, n), F32),
-            jax.ShapeDtypeStruct((8, hid), F32),
-            jax.ShapeDtypeStruct((hid, feat), F32),
-            jax.ShapeDtypeStruct(fac.shape, BF16),
+            jax.ShapeDtypeStruct((16, 8, hid // 128, 2 * feat), BF16),
+            jax.ShapeDtypeStruct((2, KK, fac.shape[1] // 2, n), BF16),
         ),
         scratch_shapes=[pltpu.VMEM((feat, n), F32)],
         compiler_params=pltpu.CompilerParams(vmem_limit_bytes=VMEM),
@@ -315,15 +317,30 @@
 
 
 def bwd_kernel(
-    dfac, words, pooled, kron_t, tg_out, pg_out,
-    gbuf, acc, dpool, wbuf, pbuf,
+    dfac, words, pooled, kron_t, grads,
+    tg_out, hid_out, pg_out,
+    gbuf, acc, dpool, wbuf, pbuf, tbuf, t_half, t_full, t_z, pg,
+    h_core, h_sum, h_half, h_full, h_z, hx_sum, hx_half, hx_full, hx_z, p_x, p_z, p_all,
     own_sem, w_sem, p_sem, core_s, core_r, ici_s, ici_r, half_s, half_r,
+    th_s, th_r, tf_s, tf_r, tz_s, tz_r, gz_s, gz_r, gx_s, gx_r, gh_s, gh_r, h_s, h_r, q_s, q_r,
 ):
     me, core, y, z, other, right, left, across = peers()
-    barrier((other, right, left, across))
-    n_f = wbuf.shape[1]
-    emb = dfac.shape[1]
+    opposite = {"mp": z * 8 + lax.rem(y + 2, 4) * 2 + core}
+    rep = lax.axis_index("replica")
+    x = lax.rem(rep, 4)
+    zl = lax.div(rep, 4)
+    x_to = [None] + [{"replica": zl * 4 + lax.rem(x + d, 4)} for d in (1, 2, 3)]
+    x_right, x_left = x_to[1], x_to[3]
+    z_near = {"replica": (1 - zl) * 4 + x}
+    n_f = tbuf.shape[1]
+    width = dpool.shape[1]
     places = ((0, 0), (0, 3), (0, 1), (1, 0), (1, 3), (1, 1), (0, 2), (1, 2))
+    order = [(p, n) for p in range(2) for n in (0, 1, 2, 3, 6, 4, 5, 7)]
+    sends = []
+
+    def go(copy):
+        copy.start()
+        sends.append(copy)
 
     def chip(n):
         dz, dy = places[n]
@@ -332,163 +349,426 @@
     def block(n):
         return chip(n) * 2 + core
 
-    def to_core(n):
-        return remote(gbuf.at[block(n)], gbuf.at[block(n)], core_s.at[n], core_r.at[n], other)
-
-    def from_core(n):
-        j = chip(n) * 2 + 1 - core
-        return remote(gbuf.at[j], gbuf.at[j], core_s.at[n], core_r.at[n], other)
-
-    def whole(n, m, device):
-        j = block(n)
-        return remote(gbuf.at[j], gbuf.at[j], ici_s.at[m], ici_r.at[m], device)
-
-    def arrived(m):
-        j = block(m)
-        remote(gbuf.at[j], gbuf.at[j], ici_s.at[m], ici_r.at[m], right).wait_recv()
-
-    def half(n, m, d):
-        j = block(n)
-        part = pl.ds(d * K1, K1)
-        i = (m - 6, d)
-        return remote(gbuf.at[j, part], gbuf.at[j, part], half_s.at[i], half_r.at[i], (right, left)[d])
-
-    def half_arrived(m, d):
-        j = block(m)
-        part = pl.ds(d * K1, K1)
-        i = (m - 6, d)
-        remote(gbuf.at[j, part], gbuf.at[j, part], half_s.at[i], half_r.at[i], right).wait_recv()
+    def to_core(p, n):
+        ref = gbuf.at[p, block(n)]
+        return remote(ref, ref, core_s.at[p, n], core_r.at[p, n], other)
+
+    def from_core(p, n):
+        ref = gbuf.at[p, chip(n) * 2 + 1 - core]
+        remote(ref, ref, core_s.at[p, n], core_r.at[p, n], other).wait_recv()
+
+    def whole(p, n, m, device):
+        ref = gbuf.at[p, block(n)]
+        return remote(ref, ref, ici_s.at[p, m], ici_r.at[p, m], device)
+
+    def arrived(p, m):
+        whole(p, m, m, right).wait_recv()
+
+    def half(p, n, m, d):
+        ref = gbuf.at[p, block(n), pl.ds(d * K1, K1)]
+        i = (p, m - 6, d)
+        return remote(ref, ref, half_s.at[i], half_r.at[i], (right, left)[d])
+
+    def half_arrived(p, m):
+        for d in range(2):
+            half(p, m, m, d).wait_recv()
+        go(to_core(p, m))
+
+    def near(p):
+        arrived(p, 1)
+        go(half(p, 1, 6, 0))
+        go(to_core(p, 1))
+        arrived(p, 2)
+        go(half(p, 2, 6, 1))
+        go(to_core(p, 2))
+        arrived(p, 3)
+        go(whole(p, 3, 4, right))
+        go(whole(p, 3, 5, left))
+        go(to_core(p, 3))
+
+    def far(p):
+        arrived(p, 4)
+        go(half(p, 4, 7, 0))
+        go(to_core(p, 4))
+        arrived(p, 5)
+        go(half(p, 5, 7, 1))
+        go(to_core(p, 5))
 
     def w_copy(n):
-        return pltpu.make_async_copy(words.at[chip(n)], wbuf.at[n % 2], w_sem.at[n % 2])
-
-    def p_copy(n):
-        return pltpu.make_async_copy(pooled.at[chip(n)], pbuf.at[n % 2], p_sem.at[n % 2])
-
-    w_copy(0).start()
-    p_copy(0).start()
-    own = pltpu.make_async_copy(dfac, gbuf.at[me], own_sem)
-    own.start()
-    own.wait()
-    sends = [whole(0, 1, right), whole(0, 2, left), whole(0, 3, across), to_core(0)]
-    for s in sends:
-        s.start()
-
-    pg_out[...] = jnp.zeros_like(pg_out)
-
-    def work(n, first):
-        w_copy(n).wait()
-        p_copy(n).wait()
-        if n + 1 < 8:
-            w_copy(n + 1).start()
-            p_copy(n + 1).start()
-        slot = n % 2
+        return pltpu.make_async_copy(words.at[chip(n)], wbuf.at[n], w_sem.at[n])
+
+    def p_copy(i):
+        p, n = order[i]
+        return pltpu.make_async_copy(
+            pooled.at[chip(n), :, pl.ds(p * width, width), :], pbuf.at[i % 2], p_sem.at[i % 2]
+        )
+
+    def work(p, n):
+        i = order.index((p, n))
+        p_copy(i).wait()
+        if i + 1 < len(order):
+            p_copy(i + 1).start()
+        if p == 0:
+            w_copy(n).wait()
+        from_core(p, n)
+        slot = i % 2
         base = chip(n) * 2
 
         def spread(eb, carry):
             rows = pl.ds(pl.multiple_of(eb * SUB, SUB), SUB)
             g = jnp.concatenate(
-                [gbuf[base, :, rows, :].reshape(KK * SUB, 128), gbuf[base + 1, :, rows, :].reshape(KK * SUB, 128)],
-                axis=1,
+                [gbuf[p, base + c, :, rows, :].reshape(KK * SUB, 128) for c in range(2)], axis=1
             )
             d = jnp.dot(kron_t[...], g, preferred_element_type=F32).astype(BF16)
             dpool[:, rows, :] = d.reshape(n_f, SUB, 256)
-            x = pbuf[slot, :, rows, :].reshape(n_f * SUB, 256)
-            pg_out[...] += nt(x, g)
+            pg[...] += nt(pbuf[slot, :, rows, :].reshape(n_f * SUB, 256), g)
             return carry
 
-        lax.fori_loop(0, emb // SUB, spread, 0)
+        lax.fori_loop(0, width // SUB, spread, 0, unroll=4)
 
         def field(f, carry):
-            part = nt(digits(wbuf[slot, f]), dpool[f])
-            if first:
+            part = nt(digits(wbuf[n, f]), dpool[f])
+            if n == 0:
                 acc[f] = part
             elif n == 7:
-                tg_out[f] = (acc[f] + part).astype(BF16)
+                tbuf[p, f] = (acc[f] + part).astype(BF16)
             else:
                 acc[f] += part
             return carry
 
-        lax.fori_loop(0, n_f, field, 0)
-
-    def go(copy):
-        copy.start()
-        sends.append(copy)
-
-    from_core(0).wait_recv()
-    work(0, True)
-    arrived(1)
-    go(half(1, 6, 0))
-    go(to_core(1))
-    arrived(2)
-    go(half(2, 6, 1))
-    go(to_core(2))
-    arrived(3)
-    go(whole(3, 4, right))
-    go(whole(3, 5, left))
-    go(to_core(3))
-    from_core(1).wait_recv()
-    work(1, False)
-    from_core(2).wait_recv()
-    work(2, False)
-    for d in range(2):
-        half_arrived(6, d)
-    go(to_core(6))
-    from_core(3).wait_recv()
-    work(3, False)
-    arrived(4)
-    go(half(4, 7, 0))
-    go(to_core(4))
-    arrived(5)
-    go(half(5, 7, 1))
-    go(to_core(5))
-    from_core(4).wait_recv()
-    work(4, False)
-    from_core(5).wait_recv()
-    work(5, False)
-    from_core(6).wait_recv()
-    work(6, False)
-    for d in range(2):
-        half_arrived(7, d)
-    go(to_core(7))
-    from_core(7).wait_recv()
-    work(7, False)
+        lax.fori_loop(0, n_f, field, 0, unroll=4)
+
+    def first(dx, zo):
+        return (lax.rem(zl + 1 + zo, 2) * 4 + lax.rem(x + dx, 4)) * 2
+
+    def t_half_copy(p, zo, d):
+        i = (p, zo, d)
+        return remote(tbuf.at[p, first(2, zo) + d], t_half.at[i], th_s.at[i], th_r.at[i], (x_right, x_left)[d])
+
+    def t_full_copy(p, zo, d):
+        i = (p, zo, d)
+        src = tbuf.at[p, pl.ds(first(1 + 2 * d, zo), 2)]
+        return remote(src, t_full.at[i], tf_s.at[i], tf_r.at[i], (x_right, x_left)[d])
+
+    def t_z_copy(p):
+        return remote(tbuf.at[p, pl.ds(first(0, 0), 2)], t_z.at[p], tz_s.at[p], tz_r.at[p], z_near)
+
+    def g_x_copy(p, zb, d, dx=0):
+        ref = tg_out.at[p, pl.ds(first(dx, 1 - zb), 2)]
+        i = (p, zb, d)
+        return remote(ref, ref, gx_s.at[i], gx_r.at[i], (x_right, x_left)[d])
+
+    def g_z_copy(p, zb):
+        ref = tg_out.at[p, pl.ds(first(0, 1 - zb), 2)]
+        return remote(ref, ref, gz_s.at[p], gz_r.at[p], z_near)
+
+    def g_half_copy(p, zb, d, dx):
+        ref = tg_out.at[p, first(dx, 1 - zb) + d]
+        i = (p, zb, d)
+        return remote(ref, ref, gh_s.at[i], gh_r.at[i], (x_right, x_left)[d])
+
+    def t_start(p):
+        for zo in range(2):
+            for d in range(2):
+                go(t_half_copy(p, zo, d))
+
+    def t_pass(p, zo):
+        for d in range(2):
+            t_half_copy(p, zo, d).wait_recv()
+            at = first(1 + 2 * d, zo) + d
+            tbuf[p, at] = (tbuf[p, at].astype(F32) + t_half[p, zo, d].astype(F32)).astype(BF16)
+            go(t_full_copy(p, zo, d))
+
+    def t_total(p, zo, k):
+        total = tbuf[p, first(0, zo) + k].astype(F32)
+        return total + t_full[p, zo, 0, k].astype(F32) + t_full[p, zo, 1, k].astype(F32)
+
+    def t_cross(p):
+        for d in range(2):
+            t_full_copy(p, 0, d).wait_recv()
+        for k in range(2):
+            tbuf[p, first(0, 0) + k] = t_total(p, 0, k).astype(BF16)
+        go(t_z_copy(p))
+
+    def t_finish(p):
+        for d in range(2):
+            t_full_copy(p, 1, d).wait_recv()
+        t_z_copy(p).wait_recv()
+        for k in range(2):
+            tg_out[p, first(0, 1) + k] = (t_total(p, 1, k) + t_z[p, k].astype(F32)).astype(BF16)
+        go(g_z_copy(p, 0))
+        for d in range(2):
+            go(g_x_copy(p, 0, d))
+
+    def t_spread(p):
+        g_z_copy(p, 1).wait_recv()
+        for d in range(2):
+            go(g_x_copy(p, 1, d))
+
+    def t_relay(p, zb):
+        for d in range(2):
+            dx = 3 - 2 * d
+            g_x_copy(p, zb, d, dx).wait_recv()
+            go(g_half_copy(p, zb, d, dx))
+
+    def t_last(p):
+        for zb in range(2):
+            for d in range(2):
+                g_half_copy(p, zb, d, 2).wait_recv()
+
+    def h_copy(i):
+        if i == 0:
+            src, dst, to = grads.at[:, 1 - core], h_core, other
+        elif i < 3:
+            d = i - 1
+            src, dst, to = h_sum.at[:, lax.rem(y + 2, 4), pl.ds(d * 128, 128)], h_half.at[d], (right, left)[d]
+        elif i < 5:
+            d = i - 3
+            src, dst, to = h_sum.at[:, lax.rem(y + 1 + 2 * d, 4)], h_full.at[d], (right, left)[d]
+        elif i == 5:
+            src, dst, to = h_sum.at[1 - z, y], h_z, across
+        elif i < 8:
+            d = i - 6
+            src, dst, to = hx_sum.at[:, lax.rem(x + 2, 4), pl.ds(d * 16, 16)], hx_half.at[d], (x_right, x_left)[d]
+        elif i < 10:
+            d = i - 8
+            src, dst, to = hx_sum.at[:, lax.rem(x + 1 + 2 * d, 4)], hx_full.at[d], (x_right, x_left)[d]
+        else:
+            src, dst, to = hx_sum.at[1 - zl, x], hx_z, z_near
+        return remote(src, dst, h_s.at[i], h_r.at[i], to)
+
+    def wide(v):
+        return v.astype(F32)
+
+    def h1():
+        h_copy(0).wait_recv()
+        for q in range(8):
+            total = wide(grads[q, core]) + wide(h_core[q])
+            h_sum[q // 4, q % 4] = total.astype(BF16).reshape(h_sum.shape[2:])
+        go(h_copy(1))
+        go(h_copy(2))
+
+    def h2():
+        for d in range(2):
+            h_copy(1 + d).wait_recv()
+            at, rows = lax.rem(y + 1 + 2 * d, 4), pl.ds(d * 128, 128)
+            for k in range(2):
+                h_sum[k, at, rows] = (wide(h_sum[k, at, rows]) + wide(h_half[d, k])).astype(BF16)
+            go(h_copy(3 + d))
+
+    def h3():
+        for d in range(2):
+            h_copy(3 + d).wait_recv()
+        for k in range(2):
+            h_sum[k, y] = (wide(h_sum[k, y]) + wide(h_full[0, k]) + wide(h_full[1, k])).astype(BF16)
+        go(h_copy(5))
+
+    def h4():
+        h_copy(5).wait_recv()
+        total = (wide(h_sum[z, y]) + wide(h_z[...])).astype(BF16).reshape(8, 32, 128)
+        for q in range(8):
+            hx_sum[q // 4, q % 4] = total[q]
+        go(h_copy(6))
+        go(h_copy(7))
+
+    def h5():
+        for d in range(2):
+            h_copy(6 + d).wait_recv()
+            at, rows = lax.rem(x + 1 + 2 * d, 4), pl.ds(d * 16, 16)
+            for k in range(2):
+                hx_sum[k, at, rows] = (wide(hx_sum[k, at, rows]) + wide(hx_half[d, k])).astype(BF16)
+            go(h_copy(8 + d))
+
+    def h6():
+        for d in range(2):
+            h_copy(8 + d).wait_recv()
+        for k in range(2):
+            hx_sum[k, x] = (wide(hx_sum[k, x]) + wide(hx_full[0, k]) + wide(hx_full[1, k])).astype(BF16)
+        go(h_copy(10))
+
+    def h7():
+        h_copy(10).wait_recv()
+        hid_out[...] = wide(hx_sum[zl, x]) + wide(hx_z[...])
+
+    def q_copy(i):
+        if i < 3:
+            src, dst, to = p_x.at[3], p_x.at[i], x_to[1 + i]
+        elif i == 3:
+            src, dst, to = p_z.at[0], p_z.at[1], z_near
+        elif i == 4:
+            ref = p_all.at[z, y, core]
+            src, dst, to = ref, ref, other
+        elif i < 8:
+            ref = p_all.at[z, y]
+            src, dst, to = ref, ref, (right, opposite, left)[i - 5]
+        else:
+            ref = p_all.at[z]
+            src, dst, to = ref, ref, across
+        return remote(src, dst, q_s.at[i], q_r.at[i], to)
+
+    def q0():
+        a = lax.rem(lax.broadcasted_iota(jnp.int32, pg.shape, 0), SUB)
+        b = lax.rem(lax.broadcasted_iota(jnp.int32, pg.shape, 1), SUB)
+        p_x[3] = jnp.sum(jnp.where(a == b, pg[...], 0.0).reshape(n_f, SUB, KK * SUB), axis=1)
+        for i in range(3):
+            go(q_copy(i))
+
+    def q1():
+        for i in range(3):
+            q_copy(i).wait_recv()
+        p_z[0] = p_x[0] + p_x[1] + p_x[2] + p_x[3]
+        go(q_copy(3))
+
+    def q2():
+        q_copy(3).wait_recv()
+        p_all[z, y, core] = p_z[0] + p_z[1]
+        go(q_copy(4))
+
+    def q3():
+        ref = p_all.at[z, y, 1 - core]
+        remote(ref, ref, q_s.at[4], q_r.at[4], other).wait_recv()
+        for i in range(3):
+            go(q_copy(5 + i))
+
+    def q4():
+        for i in range(3):
+            ref = p_all.at[z, lax.rem(y + 3 - i, 4)]
+            remote(ref, ref, q_s.at[5 + i], q_r.at[5 + i], right).wait_recv()
+        go(q_copy(8))
+
+    def q5():
+        ref = p_all.at[1 - z]
+        remote(ref, ref, q_s.at[8], q_r.at[8], across).wait_recv()
+        j = 2 * rep + lax.div(me, 8)
+        pg_out[...] = p_all[lax.div(j, 8), lax.rem(lax.div(j, 2), 4), lax.rem(j, 2)]
+
+    own = [pltpu.make_async_copy(dfac.at[p], gbuf.at[p, me], own_sem.at[p]) for p in range(2)]
+    for c in own:
+        c.start()
+    p_copy(0).start()
+    for _, n in order[:8]:
+        w_copy(n).start()
+    pg[...] = jnp.zeros_like(pg)
+    barrier((other, right, left, opposite, across, x_to[1], x_to[2], x_to[3], z_near))
+    own[0].wait()
+    go(whole(0, 0, 1, right))
+    go(whole(0, 0, 2, left))
+    go(whole(0, 0, 3, across))
+    go(to_core(0, 0))
+    go(h_copy(0))
+    own[1].wait()
+    go(to_core(1, 0))
+    work(0, 0)
+    h1()
+    near(0)
+    go(whole(1, 0, 3, across))
+    work(0, 1)
+    h2()
+    work(0, 2)
+    work(0, 3)
+    h3()
+    half_arrived(0, 6)
+    work(0, 6)
+    h4()
+    far(0)
+    work(0, 4)
+    h5()
+    work(0, 5)
+    half_arrived(0, 7)
+    go(whole(1, 0, 1, right))
+    go(whole(1, 0, 2, left))
+    work(0, 7)
+    t_start(0)
+    h6()
+    work(1, 0)
+    t_pass(0, 0)
+    near(1)
+    t_pass(0, 1)
+    work(1, 1)
+    t_cross(0)
+    work(1, 2)
+    h7()
+    work(1, 3)
+    t_finish(0)
+    half_arrived(1, 6)
+    work(1, 6)
+    t_spread(0)
+    far(1)
+    t_relay(0, 0)
+    work(1, 4)
+    work(1, 5)
+    t_relay(0, 1)
+    half_arrived(1, 7)
+    work(1, 7)
+    t_start(1)
+    t_last(0)
+    q0()
+    t_pass(1, 0)
+    t_pass(1, 1)
+    q1()
+    q2()
+    t_cross(1)
+    q3()
+    t_finish(1)
+    q4()
+    t_spread(1)
+    t_relay(1, 0)
+    q5()
+    t_relay(1, 1)
+    t_last(1)
     for s in sends:
         s.wait_send()
 
 
-def backward(dfac, words, pooled, kron_t):
+def backward(dfac, words, pooled, kron_t, grads):
     _, n_f, emb, _ = pooled.shape
     rows = 8 * HI
+    width = emb // 2
+    n_grad = grads.shape[2]
+    grads = grads.reshape(8, 2, 8, n_grad, 128)
     dma = pltpu.SemaphoreType.DMA
     vmem = pl.BlockSpec(memory_space=pltpu.VMEM)
     hbm = pl.BlockSpec(memory_space=pl.ANY)
+    a222 = dma((2, 2, 2))
     return pl.pallas_call(
         bwd_kernel,
         out_shape=(
-            jax.ShapeDtypeStruct((n_f, rows, emb), BF16),
-            jax.ShapeDtypeStruct((n_f * SUB, KK * SUB), F32),
+            jax.ShapeDtypeStruct((2, n_f, rows, width), BF16),
+            jax.ShapeDtypeStruct((n_grad, 128), F32),
+            jax.ShapeDtypeStruct((n_f, KK * SUB), F32),
         ),
-        in_specs=[vmem, hbm, hbm, vmem],
-        out_specs=(vmem, vmem),
+        in_specs=[vmem, hbm, hbm, vmem, vmem],
+        out_specs=(vmem, vmem, vmem),
         scratch_shapes=[
-            pltpu.VMEM((16,) + dfac.shape, BF16),
-            pltpu.VMEM((n_f, rows, emb), F32),
-            pltpu.VMEM((n_f, emb, 256), BF16),
-            pltpu.VMEM((2, n_f, HI, 256), jnp.int32),
-            pltpu.VMEM((2, n_f, emb, 256), BF16),
-            dma, dma((2,)), dma((2,)), dma((8,)), dma((8,)), dma((6,)), dma((6,)), dma((2, 2)), dma((2, 2)),
+            pltpu.VMEM((2, 16, KK, width, 128), BF16),
+            pltpu.VMEM((n_f, rows, width), F32),
+            pltpu.VMEM((n_f, width, 256), BF16),
+            pltpu.VMEM((8, n_f, HI, 256), jnp.int32),
+            pltpu.VMEM((2, n_f, width, 256), BF16),
+            pltpu.VMEM((2, n_f, rows, width), BF16),
+            pltpu.VMEM((2, 2, 2, rows, width), BF16),
+            pltpu.VMEM((2, 2, 2, 2, rows, width), BF16),
+            pltpu.VMEM((2, 2, rows, width), BF16),
+            pltpu.VMEM((n_f * SUB, KK * SUB), F32),
+            pltpu.VMEM((8, 8, n_grad, 128), BF16),
+            pltpu.VMEM((2, 4, 8 * n_grad, 128), BF16),
+            pltpu.VMEM((2, 2, 4 * n_grad, 128), BF16),
+            pltpu.VMEM((2, 2, 8 * n_grad, 128), BF16),
+            pltpu.VMEM((8 * n_grad, 128), BF16),
+            pltpu.VMEM((2, 4, n_grad, 128), BF16),
+            pltpu.VMEM((2, 2, n_grad // 2, 128), BF16),
+            pltpu.VMEM((2, 2, n_grad, 128), BF16),
+            pltpu.VMEM((n_grad, 128), BF16),
+            pltpu.VMEM((4, n_f, KK * SUB), F32),
+            pltpu.VMEM((2, n_f, KK * SUB), F32),
+            pltpu.VMEM((2, 4, 2, n_f, KK * SUB), F32),
+            dma((2,)), dma((8,)), dma((2,)), dma((2, 8)), dma((2, 8)), dma((2, 6)), dma((2, 6)), a222, a222,
+            a222, a222, a222, a222, dma((2,)), dma((2,)), dma((2,)), dma((2,)), a222, a222, a222, a222,
+            dma((11,)), dma((11,)), dma((9,)), dma((9,)),
         ],
         compiler_params=pltpu.CompilerParams(collective_id=1, has_side_effects=True, vmem_limit_bytes=VMEM),
         cost_estimate=pl.CostEstimate(flops=20 * 10**9, bytes_accessed=40 * 10**6, transcendentals=0),
-    )(dfac, words, pooled, kron_t)
-
-
-def scatter_sum(x):
-    rows = x.shape[0] // 128
-    x = x.reshape(8, 16, rows, x.shape[1])
-    x = lax.all_to_all(x, "mp", 1, 1, tiled=True).sum(1)
-    return lax.all_to_all(x, "replica", 0, 0, tiled=True).sum(0)
+    )(dfac, words, pooled, kron_t, grads)
 
 
 def local(indices, lengths, tables, proj, w_hidden, w_out, d_logit):
@@ -498,17 +778,19 @@
     eye = jnp.eye(SUB, dtype=BF16)
     kron_t = (here[:, None, :, None] * eye[None, :, None, :]).reshape(n_f * SUB, KK * SUB)
     words, pooled, fac = forward(indices, lengths, tables.transpose(0, 2, 1), kron_t.T)
-    logits, out_part, hidden_part, dfac = dense(fac, w_hidden, w_out, d_logit)
-    table_part, pg = backward(dfac, words, pooled, kron_t)
-    table_grad = lax.psum(table_part, "replica").astype(F32)
-    pg = jnp.einsum("fakb,ab->fk", pg.reshape(n_f, SUB, KK, SUB), jnp.eye(SUB, dtype=F32), precision="highest")
-    pg_all = lax.dynamic_update_slice_in_dim(jnp.zeros(proj.shape, F32), pg, me * n_f, 0)
-    place = lax.axis_index("replica") * 16 + me
-    pg_all = lax.psum(pg_all, ("replica", "mp"))
-    proj_share = lax.dynamic_slice_in_dim(pg_all, place * (proj.shape[0] // 128), proj.shape[0] // 128, 0)
-    both = jnp.concatenate([hidden_part, out_part.sum(0)[:, None]], axis=1)
-    both = scatter_sum(both)
-    return (logits.reshape(-1), table_grad, both[:, :-1], both[:, -1], proj_share)
+    logits, grads, dfac = dense(fac, w_hidden, w_out, d_logit)
+    tables_sum, dense_sum, pg = backward(dfac, words, pooled, kron_t, grads)
+    table_grad = jnp.concatenate([tables_sum[0], tables_sum[1]], axis=2).astype(F32)
+    feat = w_hidden.shape[1]
+    mine = proj.shape[0] // 128
+    pg = lax.dynamic_slice_in_dim(pg, lax.rem(me * mine, n_f), mine, 0)
+    return (
+        logits.reshape(-1),
+        table_grad,
+        dense_sum[:, :feat],
+        dense_sum[:, feat : feat + 3].sum(1),
+        pg.reshape(mine, KK, SUB).sum(2),
+    )
 
 
 def solution(mesh):

time: 413 us -> 266 us (0.64)
  blocking collectives: 133 us -> 0 us
  Pallas kernels: 214 us -> 241 us
  between operations: 14.2 us -> 0.72 us
  starting transfers between devices: 10.4 us -> 0 us
  waiting for transfers between devices: 6.04 us -> 0 us
  other arithmetic: 11.2 us -> 5.52 us
  matrix products: 5.34 us -> 0 us
    psum x1 -> x0, blocking collectives: 133 us -> none  [local(): pg_all = lax.psum(pg_all, ('replica', 'mp'))]
    pallas_call x1, Pallas kernels: 101 us -> 141 us  [backward(): pl.pallas_call(bwd_kernel, out_shape=(jax.ShapeDtypeStruct((2, n_f, rows,...]
    pallas_call x1, Pallas kernels: 103 us -> 90.4 us  [forward(): pl.pallas_call(fwd_kernel, out_shape=(jax.ShapeDtypeStruct((8, n_f, HI, 2...]
    all_to_all x2 -> x0, starting transfers between devices: 10.4 us -> none  [the longest x1 5.54 us: scatter_sum(): x = lax.all_to_all(x, 'mp', 1, 1, tiled=True).sum(1)]
    all_to_all x2 -> x0, waiting for transfers between devices: 6.02 us -> none  [the longest x1 6.02 us: scatter_sum(): return lax.all_to_all(x, 'replica', 0, 0, tiled=True).sum(0)]
    dot_general x1 -> x0, matrix products: 5.34 us -> none  [local(): jnp.einsum('fakb,ab->fk', pg.reshape(n_f, SUB, KK, SUB), jnp.eye(SUB, dty...]
    unnamed x18 -> x13, local copies, waits for them, and re-layouts: 9.31 us -> 9.03 us
  transfers between devices with their start and end apart: 3 -> 0, of which waited for: 1 -> 0; matrix products, arithmetic and copies ran while one was open for 3% -> 0% of each run, Pallas kernels for 0% -> 0%
where the time goes in v2:
time: 266 us; the launch traced here: 264 us
  Pallas kernels  241 us (91%)
  local copies, waits for them, and re-layouts  16.4 us (6%)
  other arithmetic  5.52 us (2%)
    pallas_call x1, Pallas kernels, backward(): pl.pallas_call(bwd_kernel, out_shape=(jax.ShapeDtypeStruct((2, n_f, rows,...  141 us
    pallas_call x1, Pallas kernels, forward(): pl.pallas_call(fwd_kernel, out_shape=(jax.ShapeDtypeStruct((8, n_f, HI, 2...  90.4 us
    pallas_call x1, Pallas kernels, dense(): pl.pallas_call(dense_kernel, out_shape=(jax.ShapeDtypeStruct((1, n), F32)...  9.43 us
    unnamed x13, local copies, waits for them, and re-layouts  9.03 us

profile of v2, /device:TPU:0, one launch (start us, length us, event | category | flops | bytes accessed | tf_op | source)
XLA Modules:
  0.0 263.7 jit_solution(700985366182276049)
XLA Ops:
  0.6 0.0 copy-start
  0.7 0.7 copy-done
  1.3 0.1 constant_dynamic-slice_fusion.1
  1.4 0.1 copy.17
  1.5 0.1 broadcast_multiply_fusion
  1.7 1.0 mul.27.kron_t
  2.6 0.0 copy-start.2
  2.7 0.8 copy.18.kron
  3.4 6.4 %copy.16 = bf16[16,512,256]{1,2,0:T(8,128)(2,1)} copy(bf16[16,512,256]{2,1,0:T(8,128)(2,1)} %param.9) | data formatting | bytes 8388608 | tf_op args[2]
  9.8 0.0 copy-done.2
  9.8 0.0 copy-start.4
  9.8 0.0 copy-start.1
  9.8 90.4 %shard_map.110 = (s32[8,16,64,256]{3,2,1,0:T(8,128)}, bf16[8,16,256,256]{3,2,1,0:T(8,128)(2,1)}, f32[16,256,128]{2,1,0:T(8,128)}) custom-call(s32[16,8,2048]{2,1,0:T(8,128)} %idx.1, s32[16,2048]{1,0:T(8,128)} %lens.1, bf16[16,256,512]{2,1,0:T(8,128)(2,1)} %bitcast.13, bf16[256,256]{1,0:T(8,128)(2,1)} %copy.18.kron), custom_call_target="tpu_custom_call" | custom-call | flops 15000000512 | bytes 40000000 | tf_op jit(solution)/shard_map/pallas_call | solution.py:207
  100.3 0.0 copy-done.4
  100.3 1.6 broadcast_in_dim.17.wo_col
  101.9 0.0 copy-done.1
  101.9 1.3 copy.19.wh
  103.2 0.6 broadcast_in_dim.7.wo_row
  103.8 9.4 %shard_map.111 = (f32[1,128]{1,0:T(1,128)}, bf16[16,8,32,128]{3,2,1,0:T(8,128)(2,1)}, bf16[2,16,128,128]{3,2,1,0:T(8,128)(2,1)}) custom-call(f32[16,256,128]{2,1,0:T(8,128)} %get-tuple-element.14.fac, bf16[4096,64]{1,0:T(8,128)(2,1)} %copy.19.wh, bf16[64,4096]{1,0:T(8,128)(2,1)} %bitcast.14, bf16[4096,1]{1,0:T(8,128)(2,1)} %broadcast_in_dim.17.wo_col, ...), custom_call_target="tpu_custom_call" | custom-call | flops 1000000000 | bytes 10000000 | tf_op jit(solution)/shard_map/pallas_call | solution.py:306
  113.2 141.2 %shard_map.112 = (bf16[2,16,512,128]{3,2,1,0:T(8,128)(2,1)}, f32[32,128]{1,0:T(8,128)}, f32[16,256]{1,0:T(8,128)}) custom-call(bf16[2,16,128,128]{3,2,1,0:T(8,128)(2,1)} %get-tuple-element.16.dfac, s32[8,16,64,256]{3,2,1,0:T(8,128)} %get-tuple-element.17.words, bf16[8,16,256,256]{3,2,1,0:T(8,128)(2,1)} %get-tuple-element.18.pooled, ...), custom_call_target="tpu_custom_call" | custom-call | flops 20000000000 | bytes 40000000 | tf_op jit(solution)/shard_map/pallas_call | solution.py:733
  254.5 2.5 slice_bitcast_fusion.1
  257.0 0.0 copy-start.3
  257.0 4.0 %maximum_convert_fusion = f32[16,512,256]{2,1,0:T(8,128)} fusion(bf16[16,512,128]{2,1,0:T(8,128)(2,1)S(1)} %get-tuple-element.24, bf16[16,512,128]{2,1,0:T(8,128)(2,1)S(1)} %get-tuple-element.23), kind=kLoop, calls=%fused_computation | loop fusion | flops 8388608 | bytes 12582912 | tf_op jit(solution)/shard_map/convert_element_type | solution.py:783
  261.0 0.7 constant_dynamic-slice_fusion
  261.7 0.1 reshape.35
  261.8 0.7 reduce_sum.19
  262.4 0.0 copy-done.3
  262.4 0.7 slice_reduce_fusion
  263.1 0.6 copy.22
  (1 shorter events, 0.0 us)
Async XLA Ops:
  0.6 0.7 copy-start
  2.6 7.2 %copy-start.2 = (bf16[256,256]{1,0:T(8,128)(2,1)}, bf16[256,256]{1,0:T(8,128)(2,1)S(1)}, u32[]{:S(2)}) copy-start(bf16[256,256]{1,0:T(8,128)(2,1)S(1)} %mul.27.kron_t) | copy-start | bytes 393220
  9.8 90.4 %copy-start.4 = (bf16[4096]{0:T(1024)(128)(2,1)S(1)}, bf16[4096]{0:T(1024)(128)(2,1)}, u32[]{:S(2)}) copy-start(bf16[4096]{0:T(1024)(128)(2,1)} %param.12) | copy-start | bytes 24580
  9.8 92.0 %copy-start.1 = (bf16[4096,64]{0,1:T(8,128)(2,1)S(1)}, bf16[4096,64]{0,1:T(8,128)(2,1)}, u32[]{:S(2)}) copy-start(bf16[4096,64]{0,1:T(8,128)(2,1)} %param.11) | copy-start | bytes 1572868
  257.0 5.5 %copy-start.3 = (f32[32,128]{1,0:T(8,128)S(1)}, f32[32,128]{1,0:T(8,128)}, u32[]{:S(2)}) copy-start(f32[32,128]{1,0:T(8,128)} %get-tuple-element.21) | copy-start | bytes 49156

commit v3 on v2

--- a/solution.py
+++ b/solution.py
@@ -15,6 +15,9 @@
 HI = 64
 BITS = 4
 VMEM = 60 * 1024 * 1024
+LOW = 9
+LOW_HALF = 5
+GATHER_LOW = (9, 12)
 F32 = jnp.float32
 BF16 = jnp.bfloat16
 
@@ -50,24 +53,25 @@
     )
 
 
+def nt(a, b):
+    return lax.dot_general(a, b, (((1,), (1,)), ((), ())), preferred_element_type=F32)
+
+
 def fwd_kernel(
-    idx, lens, tab_t, kron, words_out, pooled_out, fac_out,
-    sbuf, rcore, rhalf, rfull, rz, wbuf, pbuf,
-    core_s, core_r, half_s, half_r, full_s, full_r, z_s, z_r, w_sem, p_sem,
+    idx, lens, tab, kron, words_out, pooled_out, fac_out,
+    tab_t, sbuf, rcore, rhalf, rfull, rz, rshare, wbuf, pbuf,
+    core_s, core_r, half_s, half_r, full_s, full_r, z_s, z_r, share_s, share_r, w_sem, p_sem,
 ):
     me, core, y, z, other, right, left, across = peers()
-    barrier((other, right, left, across))
     n_f = idx.shape[0]
-    emb = tab_t.shape[1]
-
-    def zo_of(t):
-        return jnp.where(t < 2, t, jnp.where(t < 6, lax.div(t - 2, 2), t - 6))
+    emb = tab.shape[2]
 
     def chunk_of(t):
-        dy = jnp.where(t < 2, 2, jnp.where(t < 6, 1 + 2 * lax.rem(t, 2), 0))
-        zo = zo_of(t)
-        zt = lax.rem(z + 1 + zo, 2)
-        return zt * 4 + lax.rem(y + dy, 4)
+        u = lax.rem(t, 3)
+        early = lax.div(7 - t, 2) > 0
+        dy = jnp.where(early, jnp.where(u == 0, 2, 2 * u - 1), 0)
+        zo = jnp.where(early, lax.div(t, 3), t - 6)
+        return lax.rem(z + 1 + zo, 2) * 4 + lax.rem(y + dy, 4)
 
     def p_copy(t):
         slot = lax.rem(t, 2)
@@ -79,25 +83,44 @@
     def core_copy(t):
         return remote(sbuf.at[t, 1 - core], rcore.at[t], core_s.at[t], core_r.at[t], other)
 
-    def half_copy(t, zo, d):
+    def half_range(zo, d):
+        if zo:
+            return d * K1, d * K1 + K1
+        return (0, LOW_HALF) if d == 0 else (LOW_HALF, LOW)
+
+    def half_copy(zo, d):
+        a, b = half_range(zo, d)
+        ks = pl.ds(a, b - a)
         return remote(
-            sbuf.at[t, core, pl.ds(d * K1, K1)], rhalf.at[zo, d], half_s.at[zo, d], half_r.at[zo, d], (right, left)[d]
+            sbuf.at[3 * zo, core, ks], rhalf.at[zo, ks], half_s.at[zo, d], half_r.at[zo, d], (right, left)[d]
         )
 
-    def full_copy(t, zo, d):
-        return remote(sbuf.at[t, core], rfull.at[zo, d], full_s.at[zo, d], full_r.at[zo, d], (right, left)[d])
+    def full_copy(zo, d):
+        ks = pl.ds(0, KK if zo else LOW)
+        return remote(
+            sbuf.at[3 * zo + 1 + d, core, ks], rfull.at[zo, d, ks], full_s.at[zo, d], full_r.at[zo, d], (right, left)[d]
+        )
+
+    def share_copy(t):
+        return remote(sbuf.at[t, core, pl.ds(LOW, KK - LOW)], rshare.at[t], share_s.at[t], share_r.at[t], across)
 
     def z_copy():
         return remote(sbuf.at[6, core], rz, z_s, z_r, across)
 
-    def compute(t):
+    def compute(t, start=False):
         q = chunk_of(t)
         slot = lax.rem(t, 2)
         where = pl.ds(pl.multiple_of(q * 256, 256), 256)
-
-        @pl.when(t >= 2)
-        def _():
-            p_copy(t - 2).wait()
+        if not start:
+
+            @pl.when(t >= 2)
+            def _():
+                p_copy(t - 2).wait()
+
+        else:
+            eye = (
+                lax.broadcasted_iota(jnp.int32, (emb, emb), 0) == lax.broadcasted_iota(jnp.int32, (emb, emb), 1)
+            ).astype(F32).astype(BF16)
 
         def field(f, carry):
             ids = idx[f, :, where]
@@ -110,7 +133,12 @@
             for s in range(8):
                 words = words + jnp.where(hi[s : s + 1, :] == rows, val[s : s + 1, :], 0)
             wbuf[t, f] = words
-            pooled = jnp.dot(tab_t[f], digits(words), preferred_element_type=F32)
+            if start:
+                table = nt(eye, tab[f]).astype(BF16)
+                tab_t[f] = table
+            else:
+                table = tab_t[f]
+            pooled = jnp.dot(table, digits(words), preferred_element_type=F32)
             pbuf[slot, f] = pooled.astype(BF16)
             return carry
 
@@ -127,80 +155,99 @@
             return carry
 
         lax.fori_loop(0, emb // SUB, block, 0, unroll=4)
-        core_copy(t).start()
-
-    def add(t, pairs, out=None):
-        def one(k, carry, refs):
-            total = sbuf[t, core, k].astype(F32)
-            for r, first in refs:
-                total = total + r[k - first].astype(F32)
-            if out is None:
-                sbuf[t, core, k] = total.astype(BF16)
-            else:
-                out[k] = total
+        if not start:
+            core_copy(t).start()
+
+    def add(t, parts, out=None):
+        edges = sorted({0, KK, *(e for _, _, a, b in parts for e in (a, b))})
+        for low, high in zip(edges, edges[1:]):
+            refs = [(r, base) for r, base, a, b in parts if a <= low and high <= b]
+
+            def one(k, carry, refs=refs):
+                total = sbuf[t, core, k].astype(F32)
+                for r, base in refs:
+                    total = total + r[k - base].astype(F32)
+                if out is None:
+                    sbuf[t, core, k] = total.astype(BF16)
+                else:
+                    out[k] = total
+                return carry
+
+            lax.fori_loop(low, high, one, 0)
+
+    def near(t):
+        core_copy(t).wait_recv()
+        return (rcore.at[t], 0, 0, KK)
+
+    def share(t):
+        share_copy(t).wait_recv()
+        return (rshare.at[t], LOW, LOW, KK)
+
+    def opposite(zo):
+        add(3 * zo, [near(3 * zo)] + ([share(0)] if zo else []))
+        for d in range(2):
+            half_copy(zo, d).start()
+        if not zo:
+            share_copy(0).start()
+
+    def side(zo, d):
+        t = 3 * zo + 1 + d
+        half_copy(zo, d).wait_recv()
+        add(t, [near(t), (rhalf.at[zo], 0, *half_range(zo, d))] + ([share(1 + d)] if zo else []))
+        full_copy(zo, d).start()
+        if not zo:
+            share_copy(t).start()
+
+    def own(zo):
+        for d in range(2):
+            full_copy(zo, d).wait_recv()
+        parts = [near(6 + zo)] + [(rfull.at[zo, d], 0, 0, KK if zo else LOW) for d in range(2)]
+        if zo:
+            z_copy().wait_recv()
+            add(7, parts + [(rz, 0, 0, KK)], fac_out)
+        else:
+            add(6, parts)
+            z_copy().start()
+
+    def span(a, b):
+        def step(t, carry):
+            compute(t)
             return carry
 
-        lax.fori_loop(0, K1, functools.partial(one, refs=[(r, a) for r, a, b in pairs if a < K1]), 0)
-        lax.fori_loop(K1, KK, functools.partial(one, refs=[(r, a) for r, a, b in pairs if b > K1]), 0)
-
-    def pass_on(t):
-        core_copy(t).wait_recv()
-        mine = (rcore.at[t], 0, KK)
-
-        @pl.when(t < 2)
-        def _():
-            add(t, [mine])
-            half_copy(t, zo_of(t), 0).start()
-            half_copy(t, zo_of(t), 1).start()
-
-        for d in range(2):
-
-            @pl.when(jnp.logical_or(t == 2 + d, t == 4 + d))
-            def _():
-                zo = zo_of(t)
-                half_copy(zo, zo, d).wait_recv()
-                add(t, [mine, (rhalf.at[zo, d], d * K1, d * K1 + K1)])
-                full_copy(t, zo, d).start()
-
-        @pl.when(t == 6)
-        def _():
-            for d in range(2):
-                full_copy(2 + d, 0, d).wait_recv()
-            add(t, [mine, (rfull.at[0, 0], 0, KK), (rfull.at[0, 1], 0, KK)])
-            z_copy().start()
-
-    def step(t, carry):
-        compute(t)
-
-        @pl.when(t >= 1)
-        def _():
-            pass_on(t - 1)
-
-        return carry
-
-    lax.fori_loop(0, 8, step, 0)
-    core_copy(7).wait_recv()
-    for d in range(2):
-        full_copy(4 + d, 1, d).wait_recv()
-    z_copy().wait_recv()
-    add(
-        7, [(rcore.at[7], 0, KK), (rfull.at[1, 0], 0, KK), (rfull.at[1, 1], 0, KK), (rz, 0, KK)], fac_out
-    )
+        lax.fori_loop(a, b, step, 0)
+
+    compute(0, True)
+    barrier((other, right, left, across))
+    core_copy(0).start()
+    opposite(0)
+    span(1, 3)
+    side(0, 0)
+    side(0, 1)
+    span(3, 5)
+    opposite(1)
+    span(5, 7)
+    own(0)
+    side(1, 0)
+    side(1, 1)
+    span(7, 8)
+    own(1)
 
     for t in range(8):
         core_copy(t).wait_send()
         w_copy(t).wait()
     for zo in range(2):
         for d in range(2):
-            half_copy(zo, zo, d).wait_send()
-            full_copy(2 + 2 * zo + d, zo, d).wait_send()
+            half_copy(zo, d).wait_send()
+            full_copy(zo, d).wait_send()
+    for t in range(3):
+        share_copy(t).wait_send()
     z_copy().wait_send()
     p_copy(6).wait()
     p_copy(7).wait()
 
 
-def forward(indices, lengths, tab_t, kron):
-    n_f, emb, _ = tab_t.shape
+def forward(indices, lengths, tables, kron):
+    n_f, _, emb = tables.shape
     dma = pltpu.SemaphoreType.DMA
     vmem = pl.BlockSpec(memory_space=pltpu.VMEM)
     hbm = pl.BlockSpec(memory_space=pl.ANY)
@@ -214,22 +261,21 @@
         in_specs=[vmem] * 4,
         out_specs=(hbm, hbm, vmem),
         scratch_shapes=[
+            pltpu.VMEM((n_f, emb, 8 * HI), BF16),
             pltpu.VMEM((8, 2, KK, emb, 128), BF16),
             pltpu.VMEM((8, KK, emb, 128), BF16),
-            pltpu.VMEM((2, 2, K1, emb, 128), BF16),
+            pltpu.VMEM((2, KK, emb, 128), BF16),
             pltpu.VMEM((2, 2, KK, emb, 128), BF16),
             pltpu.VMEM((KK, emb, 128), BF16),
+            pltpu.VMEM((3, KK - LOW, emb, 128), BF16),
             pltpu.VMEM((8, n_f, HI, 256), jnp.int32),
             pltpu.VMEM((2, n_f, emb, 256), BF16),
-            dma((8,)), dma((8,)), dma((2, 2)), dma((2, 2)), dma((2, 2)), dma((2, 2)), dma, dma, dma((8,)), dma((2,)),
+            dma((8,)), dma((8,)), dma((2, 2)), dma((2, 2)), dma((2, 2)), dma((2, 2)), dma, dma, dma((3,)), dma((3,)),
+            dma((8,)), dma((2,)),
         ],
         compiler_params=pltpu.CompilerParams(collective_id=0, has_side_effects=True, vmem_limit_bytes=VMEM),
         cost_estimate=pl.CostEstimate(flops=15 * 10**9, bytes_accessed=40 * 10**6, transcendentals=0),
-    )(indices, lengths, tab_t, kron)
-
-
-def nt(a, b):
-    return lax.dot_general(a, b, (((1,), (1,)), ((), ())), preferred_element_type=F32)
+    )(indices, lengths, tables, kron)
 
 
 def dense_kernel(fac, wh, wh_t, wo_col, wo_row, dl, logits, grads, dfac, inter):
@@ -321,7 +367,7 @@
     tg_out, hid_out, pg_out,
     gbuf, acc, dpool, wbuf, pbuf, tbuf, t_half, t_full, t_z, pg,
     h_core, h_sum, h_half, h_full, h_z, hx_sum, hx_half, hx_full, hx_z, p_x, p_z, p_all,
-    own_sem, w_sem, p_sem, core_s, core_r, ici_s, ici_r, half_s, half_r,
+    own_sem, w_sem, p_sem, core_s, core_r, ici_s, ici_r, half_s, half_r, rest_s, rest_r,
     th_s, th_r, tf_s, tf_r, tz_s, tz_r, gz_s, gz_r, gx_s, gx_r, gh_s, gh_r, h_s, h_r, q_s, q_r,
 ):
     me, core, y, z, other, right, left, across = peers()
@@ -358,41 +404,55 @@
         remote(ref, ref, core_s.at[p, n], core_r.at[p, n], other).wait_recv()
 
     def whole(p, n, m, device):
-        ref = gbuf.at[p, block(n)]
+        ref = gbuf.at[p, block(n), pl.ds(0, GATHER_LOW[p] if m in (4, 5) else KK)]
         return remote(ref, ref, ici_s.at[p, m], ici_r.at[p, m], device)
 
     def arrived(p, m):
         whole(p, m, m, right).wait_recv()
 
     def half(p, n, m, d):
-        ref = gbuf.at[p, block(n), pl.ds(d * K1, K1)]
+        cut, top = (K1, KK) if m == 6 else ((GATHER_LOW[p] + 1) // 2, GATHER_LOW[p])
+        ref = gbuf.at[p, block(n), pl.ds(cut, top - cut) if d else pl.ds(0, cut)]
         i = (p, m - 6, d)
         return remote(ref, ref, half_s.at[i], half_r.at[i], (right, left)[d])
 
+    def rest(p, n):
+        ref = gbuf.at[p, block(n), pl.ds(GATHER_LOW[p], KK - GATHER_LOW[p])]
+        i = (1, 2, 6).index(n)
+        return remote(ref, ref, rest_s.at[p, i], rest_r.at[p, i], across)
+
+    def rest_arrived(p, m):
+        ref = gbuf.at[p, block(m), pl.ds(GATHER_LOW[p], KK - GATHER_LOW[p])]
+        i = (4, 5, 7).index(m)
+        remote(ref, ref, rest_s.at[p, i], rest_r.at[p, i], across).wait_recv()
+
     def half_arrived(p, m):
         for d in range(2):
             half(p, m, m, d).wait_recv()
+        if m == 6:
+            go(rest(p, 6))
+        else:
+            rest_arrived(p, 7)
         go(to_core(p, m))
 
     def near(p):
-        arrived(p, 1)
-        go(half(p, 1, 6, 0))
-        go(to_core(p, 1))
-        arrived(p, 2)
-        go(half(p, 2, 6, 1))
-        go(to_core(p, 2))
+        for d in range(2):
+            arrived(p, 1 + d)
+            go(half(p, 1 + d, 6, d))
+            go(rest(p, 1 + d))
+            go(to_core(p, 1 + d))
         arrived(p, 3)
         go(whole(p, 3, 4, right))
         go(whole(p, 3, 5, left))
         go(to_core(p, 3))
 
     def far(p):
-        arrived(p, 4)
-        go(half(p, 4, 7, 0))
-        go(to_core(p, 4))
-        arrived(p, 5)
-        go(half(p, 5, 7, 1))
-        go(to_core(p, 5))
+        for d in range(2):
+            arrived(p, 4 + d)
+            go(half(p, 4 + d, 7, d))
+        for d in range(2):
+            rest_arrived(p, 4 + d)
+            go(to_core(p, 4 + d))
 
     def w_copy(n):
         return pltpu.make_async_copy(words.at[chip(n)], wbuf.at[n], w_sem.at[n])
@@ -763,6 +823,7 @@
             pltpu.VMEM((2, n_f, KK * SUB), F32),
             pltpu.VMEM((2, 4, 2, n_f, KK * SUB), F32),
             dma((2,)), dma((8,)), dma((2,)), dma((2, 8)), dma((2, 8)), dma((2, 6)), dma((2, 6)), a222, a222,
+            dma((2, 3)), dma((2, 3)),
             a222, a222, a222, a222, dma((2,)), dma((2,)), dma((2,)), dma((2,)), a222, a222, a222, a222,
             dma((11,)), dma((11,)), dma((9,)), dma((9,)),
         ],
@@ -777,7 +838,7 @@
     here = lax.dynamic_slice_in_dim(proj, me * n_f, n_f, 0)
     eye = jnp.eye(SUB, dtype=BF16)
     kron_t = (here[:, None, :, None] * eye[None, :, None, :]).reshape(n_f * SUB, KK * SUB)
-    words, pooled, fac = forward(indices, lengths, tables.transpose(0, 2, 1), kron_t.T)
+    words, pooled, fac = forward(indices, lengths, tables, kron_t.T)
     logits, grads, dfac = dense(fac, w_hidden, w_out, d_logit)
     tables_sum, dense_sum, pg = backward(dfac, words, pooled, kron_t, grads)
     table_grad = jnp.concatenate([tables_sum[0], tables_sum[1]], axis=2).astype(F32)

time: 266 us -> 252 us (0.947)
  Pallas kernels: 241 us -> 230 us
  local copies, waits for them, and re-layouts: 16.4 us -> 13.2 us
    pallas_call x1, Pallas kernels: 90.4 us -> 78.9 us  [forward(): pl.pallas_call(fwd_kernel, out_shape=(jax.ShapeDtypeStruct((8, n_f, HI, 2...]
    unnamed x13 -> x10, local copies, waits for them, and re-layouts: 9.03 us -> 3.65 us
where the time goes in v3:
time: 252 us; the launch traced here: 251 us
  Pallas kernels  230 us (91%)
  local copies, waits for them, and re-layouts  13.2 us (5%)
  other arithmetic  7.16 us (3%)
    pallas_call x1, Pallas kernels, backward(): pl.pallas_call(bwd_kernel, out_shape=(jax.ShapeDtypeStruct((2, n_f, rows,...  142 us
    pallas_call x1, Pallas kernels, forward(): pl.pallas_call(fwd_kernel, out_shape=(jax.ShapeDtypeStruct((8, n_f, HI, 2...  78.9 us
    pallas_call x1, Pallas kernels, dense(): pl.pallas_call(dense_kernel, out_shape=(jax.ShapeDtypeStruct((1, n), F32)...  9.44 us
    convert_element_type x1, other arithmetic, local(): jnp.concatenate([tables_sum[0], tables_sum[1]], axis=2).astype(F32)  5.67 us

profile of v3, /device:TPU:0, one launch (start us, length us, event | category | flops | bytes accessed | tf_op | source)
XLA Modules:
  0.0 251.5 jit_solution(114401331024189235)
XLA Ops:
  0.6 0.0 copy-start
  0.6 0.0 copy-start.3
  0.7 0.7 copy-done
  1.3 0.1 constant_dynamic-slice_fusion.1
  1.4 0.1 copy.15
  1.5 1.3 broadcast_in_dim.7.wo_row
  2.8 0.1 broadcast_multiply_fusion
  3.0 1.0 mul.27.kron_t
  4.0 0.0 copy-start.1
  4.0 0.7 copy.16.kron
  4.7 2.4 copy.17.wh
  7.1 0.0 copy-done.3
  7.1 1.6 broadcast_in_dim.17.wo_col
  8.7 78.9 %shard_map.110 = (s32[8,16,64,256]{3,2,1,0:T(8,128)}, bf16[8,16,256,256]{3,2,1,0:T(8,128)(2,1)}, f32[16,256,128]{2,1,0:T(8,128)}) custom-call(s32[16,8,2048]{2,1,0:T(8,128)} %idx.1, s32[16,2048]{1,0:T(8,128)} %lens.1, bf16[16,512,256]{2,1,0:T(8,128)(2,1)} %tab.1, bf16[256,256]{1,0:T(8,128)(2,1)} %copy.16.kron), custom_call_target="tpu_custom_call" | custom-call | flops 15000000512 | bytes 40000000 | tf_op jit(solution)/shard_map/pallas_call | solution.py:254
  87.6 0.0 copy-done.1
  87.6 9.4 %shard_map.111 = (f32[1,128]{1,0:T(1,128)}, bf16[16,8,32,128]{3,2,1,0:T(8,128)(2,1)}, bf16[2,16,128,128]{3,2,1,0:T(8,128)(2,1)}) custom-call(f32[16,256,128]{2,1,0:T(8,128)} %get-tuple-element.14.fac, bf16[4096,64]{1,0:T(8,128)(2,1)} %copy.17.wh, bf16[64,4096]{1,0:T(8,128)(2,1)} %bitcast.12, bf16[4096,1]{1,0:T(8,128)(2,1)} %broadcast_in_dim.17.wo_col, ...), custom_call_target="tpu_custom_call" | custom-call | flops 1000000000 | bytes 10000000 | tf_op jit(solution)/shard_map/pallas_call | solution.py:352
  97.0 142.1 %shard_map.112 = (bf16[2,16,512,128]{3,2,1,0:T(8,128)(2,1)}, f32[32,128]{1,0:T(8,128)}, f32[16,256]{1,0:T(8,128)}) custom-call(bf16[2,16,128,128]{3,2,1,0:T(8,128)(2,1)} %get-tuple-element.16.dfac, s32[8,16,64,256]{3,2,1,0:T(8,128)} %get-tuple-element.17.words, bf16[8,16,256,256]{3,2,1,0:T(8,128)(2,1)} %get-tuple-element.18.pooled, ...), custom_call_target="tpu_custom_call" | custom-call | flops 20000000000 | bytes 40000000 | tf_op jit(solution)/shard_map/pallas_call | solution.py:793
  239.1 0.0 copy-start.2
  239.1 3.9 %slice_bitcast_fusion.1 = (bf16[16,512,128]{2,1,0:T(8,128)(2,1)S(1)}, bf16[16,512,128]{2,1,0:T(8,128)(2,1)}) fusion(bf16[2,16,512,128]{3,2,1,0:T(8,128)(2,1)} %get-tuple-element.20), kind=kLoop, calls=%fused_computation.2 | loop fusion | bytes 8388608 | tf_op jit(solution)/shard_map/squeeze | solution.py:844
  243.1 0.0 copy-done.2
  243.1 0.7 slice_reduce_fusion
  243.8 0.7 constant_dynamic-slice_fusion
  244.5 0.1 reshape.35
  244.5 0.7 reduce_sum.19
  245.2 5.7 %maximum_convert_fusion = f32[16,512,256]{2,1,0:T(8,128)} fusion(bf16[16,512,128]{2,1,0:T(8,128)(2,1)} %get-tuple-element.24, bf16[16,512,128]{2,1,0:T(8,128)(2,1)S(1)} %get-tuple-element.23), kind=kLoop, calls=%fused_computation | loop fusion | flops 8388608 | bytes 12582912 | tf_op jit(solution)/shard_map/convert_element_type | solution.py:844
  250.9 0.6 copy.20
  (1 shorter events, 0.0 us)
Async XLA Ops:
  0.6 0.7 copy-start
  0.6 6.4 %copy-start.3 = (bf16[4096]{0:T(1024)(128)(2,1)S(1)}, bf16[4096]{0:T(1024)(128)(2,1)}, u32[]{:S(2)}) copy-start(bf16[4096]{0:T(1024)(128)(2,1)} %param.12) | copy-start | bytes 24580
  4.0 83.6 %copy-start.1 = (bf16[256,256]{1,0:T(8,128)(2,1)}, bf16[256,256]{1,0:T(8,128)(2,1)S(1)}, u32[]{:S(2)}) copy-start(bf16[256,256]{1,0:T(8,128)(2,1)S(1)} %mul.27.kron_t) | copy-start | bytes 393220
  239.1 4.0 %copy-start.2 = (f32[32,128]{1,0:T(8,128)S(1)}, f32[32,128]{1,0:T(8,128)}, u32[]{:S(2)}) copy-start(f32[32,128]{1,0:T(8,128)} %get-tuple-element.21) | copy-start | bytes 49156

commit v4 on v3

--- a/solution.py
+++ b/solution.py
@@ -57,9 +57,24 @@
     return lax.dot_general(a, b, (((1,), (1,)), ((), ())), preferred_element_type=F32)
 
 
+def tn(a, b):
+    return lax.dot_general(a, b, (((0,), (0,)), ((), ())), preferred_element_type=F32)
+
+
+def spread_out(here, flip):
+    n = here.shape[0] * SUB
+    owner = lax.div(lax.broadcasted_iota(jnp.int32, (n, KK), 0), SUB)
+    pick = (owner == lax.broadcasted_iota(jnp.int32, (n, KK), 1)).astype(F32).astype(BF16)
+    rows = (nt(pick, here) if flip else jnp.dot(pick, here, preferred_element_type=F32)).astype(BF16)
+    full = nt(rows, pick)
+    a = lax.rem(lax.broadcasted_iota(jnp.int32, (n, n), 0), SUB)
+    b = lax.rem(lax.broadcasted_iota(jnp.int32, (n, n), 1), SUB)
+    return jnp.where(a == b, full, 0.0).astype(BF16)
+
+
 def fwd_kernel(
-    idx, lens, tab, kron, words_out, pooled_out, fac_out,
-    tab_t, sbuf, rcore, rhalf, rfull, rz, rshare, wbuf, pbuf,
+    idx, lens, tab, proj, words_out, pooled_out, fac_out,
+    kron, tab_t, sbuf, rcore, rhalf, rfull, rz, rshare, wbuf, pbuf,
     core_s, core_r, half_s, half_r, full_s, full_r, z_s, z_r, share_s, share_r, w_sem, p_sem,
 ):
     me, core, y, z, other, right, left, across = peers()
@@ -216,6 +231,7 @@
 
         lax.fori_loop(a, b, step, 0)
 
+    kron[...] = spread_out(proj[pl.ds(pl.multiple_of(me * n_f, n_f), n_f), :], True)
     compute(0, True)
     barrier((other, right, left, across))
     core_copy(0).start()
@@ -246,7 +262,7 @@
     p_copy(7).wait()
 
 
-def forward(indices, lengths, tables, kron):
+def forward(indices, lengths, tables, proj):
     n_f, _, emb = tables.shape
     dma = pltpu.SemaphoreType.DMA
     vmem = pl.BlockSpec(memory_space=pltpu.VMEM)
@@ -261,6 +277,7 @@
         in_specs=[vmem] * 4,
         out_specs=(hbm, hbm, vmem),
         scratch_shapes=[
+            pltpu.VMEM((n_f * SUB, KK * SUB), BF16),
             pltpu.VMEM((n_f, emb, 8 * HI), BF16),
             pltpu.VMEM((8, 2, KK, emb, 128), BF16),
             pltpu.VMEM((8, KK, emb, 128), BF16),
@@ -275,11 +292,11 @@
         ],
         compiler_params=pltpu.CompilerParams(collective_id=0, has_side_effects=True, vmem_limit_bytes=VMEM),
         cost_estimate=pl.CostEstimate(flops=15 * 10**9, bytes_accessed=40 * 10**6, transcendentals=0),
-    )(indices, lengths, tables, kron)
-
-
-def dense_kernel(fac, wh, wh_t, wo_col, wo_row, dl, logits, grads, dfac, inter):
-    hid, n_feat = wh.shape
+    )(indices, lengths, tables, proj)
+
+
+def dense_kernel(fac, wh_t, wo_row, dl, logits, grads, dfac, inter):
+    n_feat, hid = wh_t.shape
     emb = fac.shape[1]
     step = grads.shape[0] * grads.shape[2]
 
@@ -304,18 +321,23 @@
     nil = jnp.zeros((n_feat, n), BF16)
     feat_low = jnp.concatenate([feat, nil], axis=0)
     d_high = jnp.concatenate([nil, d_rows], axis=0)
+    ones = jnp.ones((8, n), BF16)
 
     def top(c, carry):
         logit_acc, d_inter = carry
         at = pl.ds(pl.multiple_of(c * step, step), step)
-        v = jnp.dot(wh[at, :], feat, preferred_element_type=F32)
+        w = wh_t[:, at]
+        v = tn(w, feat)
+        wo = jnp.broadcast_to(wo_row[:, at].astype(F32), (8, step))
+        top_row = lax.broadcasted_iota(jnp.int32, (8, step), 0) == 0
+        wo_cols = tn(jnp.where(top_row, wo, 0.0).astype(BF16), ones)
         s = jax.nn.sigmoid(v)
         hidden = (v * s).astype(BF16)
-        logit_acc = logit_acc + jnp.dot(wo_row[:, at], hidden, preferred_element_type=F32)
-        d_hidden = (wo_col[at, :].astype(F32) * row * s * (1.0 + v * (1.0 - s))).astype(BF16)
+        logit_acc = logit_acc + jnp.dot(wo.astype(BF16), hidden, preferred_element_type=F32)
+        d_hidden = (wo_cols * row * s * (1.0 + v * (1.0 - s))).astype(BF16)
         grad = nt(d_hidden, feat_low) + nt(hidden, d_high)
         grads[:, pl.ds(c, 1), :, :] = grad.astype(BF16).reshape(grads.shape[0], 1, grads.shape[2], 2 * n_feat)
-        d_inter = d_inter + jnp.dot(wh_t[:, at], d_hidden, preferred_element_type=F32)
+        d_inter = d_inter + jnp.dot(w, d_hidden, preferred_element_type=F32)
         return logit_acc, d_inter
 
     logit_acc, d_inter = lax.fori_loop(
@@ -348,7 +370,6 @@
 def dense(fac, w_hidden, w_out, d_logit):
     hid, feat = w_hidden.shape
     n = d_logit.shape[0]
-    wo_row = jnp.broadcast_to(w_out[None, :], (8, hid))
     return pl.pallas_call(
         dense_kernel,
         out_shape=(
@@ -359,13 +380,13 @@
         scratch_shapes=[pltpu.VMEM((feat, n), F32)],
         compiler_params=pltpu.CompilerParams(vmem_limit_bytes=VMEM),
         cost_estimate=pl.CostEstimate(flops=10**9, bytes_accessed=10**7, transcendentals=10**6),
-    )(fac, w_hidden, w_hidden.T, w_out[:, None], wo_row, d_logit[None, :])
+    )(fac, w_hidden.T, w_out[None, :], d_logit[None, :])
 
 
 def bwd_kernel(
-    dfac, words, pooled, kron_t, grads,
-    tg_out, hid_out, pg_out,
-    gbuf, acc, dpool, wbuf, pbuf, tbuf, t_half, t_full, t_z, pg,
+    dfac, words, pooled, proj, grads,
+    tg_low, tg_high, hid_out, pg_out,
+    kron_t, gbuf, acc, dpool, wbuf, pbuf, tbuf, t_half, t_full, t_z, pg,
     h_core, h_sum, h_half, h_full, h_z, hx_sum, hx_half, hx_full, hx_z, p_x, p_z, p_all,
     own_sem, w_sem, p_sem, core_s, core_r, ici_s, ici_r, half_s, half_r, rest_s, rest_r,
     th_s, th_r, tf_s, tf_r, tz_s, tz_r, gz_s, gz_r, gx_s, gx_r, gh_s, gh_r, h_s, h_r, q_s, q_r,
@@ -383,6 +404,7 @@
     places = ((0, 0), (0, 3), (0, 1), (1, 0), (1, 3), (1, 1), (0, 2), (1, 2))
     order = [(p, n) for p in range(2) for n in (0, 1, 2, 3, 6, 4, 5, 7)]
     sends = []
+    tg_out = (tg_low, tg_high)
 
     def go(copy):
         copy.start()
@@ -514,16 +536,16 @@
         return remote(tbuf.at[p, pl.ds(first(0, 0), 2)], t_z.at[p], tz_s.at[p], tz_r.at[p], z_near)
 
     def g_x_copy(p, zb, d, dx=0):
-        ref = tg_out.at[p, pl.ds(first(dx, 1 - zb), 2)]
+        ref = tg_out[p].at[pl.ds(first(dx, 1 - zb), 2)]
         i = (p, zb, d)
         return remote(ref, ref, gx_s.at[i], gx_r.at[i], (x_right, x_left)[d])
 
     def g_z_copy(p, zb):
-        ref = tg_out.at[p, pl.ds(first(0, 1 - zb), 2)]
+        ref = tg_out[p].at[pl.ds(first(0, 1 - zb), 2)]
         return remote(ref, ref, gz_s.at[p], gz_r.at[p], z_near)
 
     def g_half_copy(p, zb, d, dx):
-        ref = tg_out.at[p, first(dx, 1 - zb) + d]
+        ref = tg_out[p].at[first(dx, 1 - zb) + d]
         i = (p, zb, d)
         return remote(ref, ref, gh_s.at[i], gh_r.at[i], (x_right, x_left)[d])
 
@@ -555,7 +577,7 @@
             t_full_copy(p, 1, d).wait_recv()
         t_z_copy(p).wait_recv()
         for k in range(2):
-            tg_out[p, first(0, 1) + k] = (t_total(p, 1, k) + t_z[p, k].astype(F32)).astype(BF16)
+            tg_out[p][first(0, 1) + k] = (t_total(p, 1, k) + t_z[p, k].astype(F32)).astype(BF16)
         go(g_z_copy(p, 0))
         for d in range(2):
             go(g_x_copy(p, 0, d))
@@ -709,37 +731,30 @@
     for _, n in order[:8]:
         w_copy(n).start()
     pg[...] = jnp.zeros_like(pg)
+    kron_t[...] = spread_out(proj[pl.ds(pl.multiple_of(me * n_f, n_f), n_f), :], False)
     barrier((other, right, left, opposite, across, x_to[1], x_to[2], x_to[3], z_near))
     own[0].wait()
-    go(whole(0, 0, 1, right))
-    go(whole(0, 0, 2, left))
-    go(whole(0, 0, 3, across))
+    for i, to in enumerate((right, left, across)):
+        go(whole(0, 0, 1 + i, to))
     go(to_core(0, 0))
-    go(h_copy(0))
     own[1].wait()
     go(to_core(1, 0))
+    go(h_copy(0))
     work(0, 0)
-    h1()
     near(0)
-    go(whole(1, 0, 3, across))
     work(0, 1)
-    h2()
     work(0, 2)
     work(0, 3)
-    h3()
     half_arrived(0, 6)
     work(0, 6)
-    h4()
     far(0)
+    for i, to in enumerate((right, left, across)):
+        go(whole(1, 0, 1 + i, to))
     work(0, 4)
-    h5()
     work(0, 5)
     half_arrived(0, 7)
-    go(whole(1, 0, 1, right))
-    go(whole(1, 0, 2, left))
     work(0, 7)
     t_start(0)
-    h6()
     work(1, 0)
     t_pass(0, 0)
     near(1)
@@ -747,40 +762,46 @@
     work(1, 1)
     t_cross(0)
     work(1, 2)
-    h7()
+    half_arrived(1, 6)
     work(1, 3)
     t_finish(0)
-    half_arrived(1, 6)
+    far(1)
     work(1, 6)
     t_spread(0)
-    far(1)
+    work(1, 4)
     t_relay(0, 0)
-    work(1, 4)
     work(1, 5)
+    half_arrived(1, 7)
     t_relay(0, 1)
-    half_arrived(1, 7)
+    h1()
     work(1, 7)
     t_start(1)
+    q0()
     t_last(0)
-    q0()
+    h2()
     t_pass(1, 0)
+    q1()
     t_pass(1, 1)
-    q1()
+    h3()
     q2()
     t_cross(1)
+    h4()
     q3()
     t_finish(1)
+    h5()
     q4()
     t_spread(1)
+    h6()
     t_relay(1, 0)
     q5()
+    h7()
     t_relay(1, 1)
     t_last(1)
     for s in sends:
         s.wait_send()
 
 
-def backward(dfac, words, pooled, kron_t, grads):
+def backward(dfac, words, pooled, proj, grads):
     _, n_f, emb, _ = pooled.shape
     rows = 8 * HI
     width = emb // 2
@@ -793,13 +814,15 @@
     return pl.pallas_call(
         bwd_kernel,
         out_shape=(
-            jax.ShapeDtypeStruct((2, n_f, rows, width), BF16),
+            jax.ShapeDtypeStruct((n_f, rows, width), BF16),
+            jax.ShapeDtypeStruct((n_f, rows, width), BF16),
             jax.ShapeDtypeStruct((n_grad, 128), F32),
             jax.ShapeDtypeStruct((n_f, KK * SUB), F32),
         ),
         in_specs=[vmem, hbm, hbm, vmem, vmem],
-        out_specs=(vmem, vmem, vmem),
+        out_specs=(vmem, vmem, vmem, vmem),
         scratch_shapes=[
+            pltpu.VMEM((n_f * SUB, KK * SUB), BF16),
             pltpu.VMEM((2, 16, KK, width, 128), BF16),
             pltpu.VMEM((n_f, rows, width), F32),
             pltpu.VMEM((n_f, width, 256), BF16),
@@ -829,19 +852,16 @@
         ],
         compiler_params=pltpu.CompilerParams(collective_id=1, has_side_effects=True, vmem_limit_bytes=VMEM),
         cost_estimate=pl.CostEstimate(flops=20 * 10**9, bytes_accessed=40 * 10**6, transcendentals=0),
-    )(dfac, words, pooled, kron_t, grads)
+    )(dfac, words, pooled, proj, grads)
 
 
 def local(indices, lengths, tables, proj, w_hidden, w_out, d_logit):
     n_f = indices.shape[0]
     me = lax.axis_index("mp")
-    here = lax.dynamic_slice_in_dim(proj, me * n_f, n_f, 0)
-    eye = jnp.eye(SUB, dtype=BF16)
-    kron_t = (here[:, None, :, None] * eye[None, :, None, :]).reshape(n_f * SUB, KK * SUB)
-    words, pooled, fac = forward(indices, lengths, tables, kron_t.T)
+    words, pooled, fac = forward(indices, lengths, tables, proj)
     logits, grads, dfac = dense(fac, w_hidden, w_out, d_logit)
-    tables_sum, dense_sum, pg = backward(dfac, words, pooled, kron_t, grads)
-    table_grad = jnp.concatenate([tables_sum[0], tables_sum[1]], axis=2).astype(F32)
+    low, high, dense_sum, pg = backward(dfac, words, pooled, proj, grads)
+    table_grad = jnp.concatenate([low, high], axis=2).astype(F32)
     feat = w_hidden.shape[1]
     mine = proj.shape[0] // 128
     pg = lax.dynamic_slice_in_dim(pg, lax.rem(me * mine, n_f), mine, 0)

time: 252 us -> 228 us (0.905)
  Pallas kernels: 230 us -> 216 us
  local copies, waits for them, and re-layouts: 13.2 us -> 3.43 us
    pallas_call x1, Pallas kernels: 142 us -> 128 us  [backward(): pl.pallas_call(bwd_kernel, out_shape=(jax.ShapeDtypeStruct((n_f, rows, wi...]
    squeeze x1 -> x0, local copies, waits for them, and re-layouts: 3.94 us -> none  [local(): tables_sum[0]]
    convert_element_type x2 -> x1, other arithmetic: 5.68 us -> 6.24 us  [local(): table_grad = jnp.concatenate([low, high], axis=2).astype(F32)]
where the time goes in v4:
time: 228 us
  Pallas kernels  216 us (95%)
  other arithmetic  7.59 us (3%)
  local copies, waits for them, and re-layouts  3.43 us (2%)
    pallas_call x1, Pallas kernels, backward(): pl.pallas_call(bwd_kernel, out_shape=(jax.ShapeDtypeStruct((n_f, rows, wi...  128 us
    pallas_call x1, Pallas kernels, forward(): pl.pallas_call(fwd_kernel, out_shape=(jax.ShapeDtypeStruct((8, n_f, HI, 2...  79.2 us
    pallas_call x1, Pallas kernels, dense(): pl.pallas_call(dense_kernel, out_shape=(jax.ShapeDtypeStruct((1, n), F32)...  9.27 us
    convert_element_type x1, other arithmetic, local(): table_grad = jnp.concatenate([low, high], axis=2).astype(F32)  6.24 us

profile of v4, /device:TPU:0, one launch (start us, length us, event | category | flops | bytes accessed | tf_op | source)
XLA Modules:
  0.0 227.8 jit_solution(17630090753234661177)
XLA Ops:
  0.6 1.4 copy.12.proj
  2.0 0.0 copy-start.1
  2.1 79.2 %shard_map.110 = (s32[8,16,64,256]{3,2,1,0:T(8,128)}, bf16[8,16,256,256]{3,2,1,0:T(8,128)(2,1)}, f32[16,256,128]{2,1,0:T(8,128)}) custom-call(s32[16,8,2048]{2,1,0:T(8,128)} %idx.1, s32[16,2048]{1,0:T(8,128)} %lens.1, bf16[16,512,256]{2,1,0:T(8,128)(2,1)} %tab.1, bf16[256,16]{1,0:T(8,128)(2,1)} %copy.12.proj), custom_call_target="tpu_custom_call" | custom-call | flops 15000000512 | bytes 40000000 | tf_op jit(solution)/shard_map/pallas_call | solution.py:270
  81.2 0.0 copy-done.1
  81.3 0.6 broadcast_in_dim.6.wo_row
  81.9 9.3 %shard_map.111 = (f32[1,128]{1,0:T(1,128)}, bf16[16,8,32,128]{3,2,1,0:T(8,128)(2,1)}, bf16[2,16,128,128]{3,2,1,0:T(8,128)(2,1)}) custom-call(f32[16,256,128]{2,1,0:T(8,128)} %get-tuple-element.15.fac, bf16[64,4096]{1,0:T(8,128)(2,1)} %bitcast.6, bf16[1,4096]{1,0:T(2,128)(2,1)} %broadcast_in_dim.6.wo_row, f32[1,128]{1,0:T(1,128)} %bitcast.7), custom_call_target="tpu_custom_call" | custom-call | flops 1000000000 | bytes 10000000 | tf_op jit(solution)/shard_map/pallas_call | solution.py:373
  91.2 127.6 %shard_map.112 = (bf16[16,512,128]{2,1,0:T(8,128)(2,1)}, bf16[16,512,128]{2,1,0:T(8,128)(2,1)}, f32[32,128]{1,0:T(8,128)}, f32[16,256]{1,0:T(8,128)}) custom-call(bf16[2,16,128,128]{3,2,1,0:T(8,128)(2,1)} %get-tuple-element.17.dfac, s32[8,16,64,256]{3,2,1,0:T(8,128)} %get-tuple-element.18.words, bf16[8,16,256,256]{3,2,1,0:T(8,128)(2,1)} %get-tuple-element.19.pooled, ...), custom_call_target="tpu_custom_call" | custom-call | flops 20000000000 | bytes 40000000 | tf_op jit(solution)/shard_map/pallas_call | solution.py:814
  218.8 0.0 copy-start
  218.8 6.2 %maximum_convert_fusion = f32[16,512,256]{2,1,0:T(8,128)} fusion(bf16[16,512,128]{2,1,0:T(8,128)(2,1)} %get-tuple-element.22, bf16[16,512,128]{2,1,0:T(8,128)(2,1)} %get-tuple-element.21), kind=kLoop, calls=%fused_computation | loop fusion | flops 8388608 | bytes 12582912 | tf_op jit(solution)/shard_map/convert_element_type | solution.py:864
  225.0 0.0 copy-done
  225.0 0.7 slice_reduce_fusion
  225.7 0.7 constant_dynamic-slice_fusion
  226.4 0.1 reshape.21
  226.5 0.7 reduce_sum.19
  227.2 0.6 copy.15
Async XLA Ops:
  2.0 79.2 %copy-start.1 = (bf16[4096]{0:T(1024)(128)(2,1)S(1)}, bf16[4096]{0:T(1024)(128)(2,1)}, u32[]{:S(2)}) copy-start(bf16[4096]{0:T(1024)(128)(2,1)} %param.12) | copy-start | bytes 24580
  218.8 6.3 %copy-start = (f32[32,128]{1,0:T(8,128)S(1)}, f32[32,128]{1,0:T(8,128)}, u32[]{:S(2)}) copy-start(f32[32,128]{1,0:T(8,128)} %get-tuple-element.23) | copy-start | bytes 49156
